TPU v7x, 32 devices: a whole 2x2x4 slice. The times are simulated.
32 devices in a mesh: row: 4 (over z), col: 2 (over y), layer: 4 (over x, core).
Axes of the slice: x: 2, y: 2, z: 4, core: 2. Of those that a mesh axis runs over, the one named last changes fastest.
Arguments:
- left_blocks: bfloat16 [4096, 16384], P('row', ('layer', 'col')), may hold values from -6 to 6
- left_pattern: int32 [64, 256], P('row', ('layer', 'col')), may hold values 0 or 1
- right_blocks: bfloat16 [16384, 2048], P(('layer', 'col'), 'row'), may hold values from -0.125 to 0.125
- right_pattern: int32 [256, 32], P(('layer', 'col'), 'row'), may hold values 0 or 1
Outputs:
- product: bfloat16 [4096, 2048], P('row', ('col', 'layer'))
All inputs are finite; a program needn't handle non-finite values. No bound on the sum of `left_pattern` or of `right_pattern` on one device may be relied on, other than what follows from the above.
Results may differ from a plain program's by a relative error of at most 0.001.
Values may be sent and summed in bfloat16 or wider, within the bound.
A program may use at most 64 MiB of HBM per device.

v0:
```python
import jax
import jax.numpy as jnp
from jax import lax
from jax.sharding import PartitionSpec as P


def from_behind(x, axis, by):
    size = lax.axis_size(axis)
    return lax.ppermute(x, axis, [(i, (i + by) % size) for i in range(size)])


def apply_pattern(values, pattern):
    rows, cols = values.shape
    block = rows // pattern.shape[0]
    shaped = values.reshape(pattern.shape[0], block, pattern.shape[1], block)
    masked = shaped * pattern[:, None, :, None].astype(jnp.bfloat16)
    return masked.reshape(rows, cols)


def local(left_blocks, left_pattern, right_blocks, right_pattern):
    left = apply_pattern(left_blocks, left_pattern)
    right = apply_pattern(right_blocks, right_pattern)
    left_rows = left.shape[0]
    range_cols = right.shape[1]
    cycle_size = lax.axis_size("row")
    position = lax.axis_index("row")
    partial_value = jnp.zeros((left_rows, range_cols * cycle_size), jnp.float32)
    current = right
    for step in range(cycle_size):
        if step > 0:
            current = from_behind(current, "row", 1)
        owner = (position - step) % cycle_size
        piece = jnp.dot(left, current, preferred_element_type=jnp.float32)
        partial_value = lax.dynamic_update_slice_in_dim(partial_value, piece, owner * range_cols, 1)
    reduced = lax.psum_scatter(partial_value, ("col", "layer"), scatter_dimension=1, tiled=True)
    return reduced.astype(jnp.bfloat16)


def solution(mesh):
    placed = (
        P("row", ("layer", "col")),
        P("row", ("layer", "col")),
        P(("layer", "col"), "row"),
        P(("layer", "col"), "row"),
    )
    return jax.shard_map(
        local, mesh=mesh, in_specs=placed, out_specs=P("row", ("col", "layer")), check_vma=False
    )
```

profile of v0, /device:TPU:0, one launch (start us, length us, event | category | flops | bytes accessed | tf_op | source)
XLA Modules:
  0.0 249.7 jit_solution(7756436775320586893)
XLA Ops:
  6.5 0.0 reduce-scatter.2.cloned.1.call-start
  6.5 0.7 convert_element_type.12
  7.2 0.1 copy.5
  7.3 2.6 %mul.37 = bf16[32,64,8,64]{3,2,1,0:T(8,128)(2,1)} broadcast(bf16[32,8]{1,0:T(8,128)(2,1)S(1)} %copy.5), dimensions={0,2} | broadcast | bytes 2097664 | tf_op jit(solution)/shard_map/mul | solution.py:16
  9.9 5.4 %mul.38 = bf16[2048,512]{1,0:T(8,128)(2,1)S(1)} reshape(bf16[32,64,8,64]{3,2,1,0:T(8,128)(2,1)} %mul.37) | data formatting | bytes 4194304 | tf_op jit(solution)/shard_map/mul | solution.py:16
  15.3 0.0 copy-start.3
  15.3 2.2 mul.39
  17.5 0.0 copy-start.1
  17.5 1.3 copy-done.1
  18.8 3.0 %collective-permute-start = (bf16[2048,512]{1,0:T(8,128)(2,1)S(1)}, bf16[2048,512]{1,0:T(8,128)(2,1)S(1)}, u32[]{:S(2)}, u32[]{:S(2)}) collective-permute-start(bf16[2048,512]{1,0:T(8,128)(2,1)S(1)} %mul.39), channel_id=1, source_target_pairs={{0,8},{8,16},{16,24},{24,0},{1,9},{9,17},{17,25},{25,1},{2,10},{10... | collective-permute-start | bytes 6291464 | tf_op jit(solution)/shard_map/ppermute | solution.py:9
  21.8 47.7 %collective-permute-done = bf16[2048,512]{1,0:T(8,128)(2,1)S(1)} collective-permute-done((bf16[2048,512]{1,0:T(8,128)(2,1)S(1)}, bf16[2048,512]{1,0:T(8,128)(2,1)S(1)}, u32[]{:S(2)}, u32[]{:S(2)}) %collective-permute-start) | collective-permute-done | bytes 2097184 | tf_op jit(solution)/shard_map/ppermute | solution.py:9
  69.5 0.0 collective-permute-start.1
  69.5 48.7 %collective-permute-done.1 = bf16[2048,512]{1,0:T(8,128)(2,1)} collective-permute-done((bf16[2048,512]{1,0:T(8,128)(2,1)S(1)}, bf16[2048,512]{1,0:T(8,128)(2,1)}, u32[]{:S(2)}, u32[]{:S(2)}) %collective-permute-start.1) | collective-permute-done | bytes 2097184 | tf_op jit(solution)/shard_map/ppermute | solution.py:9
  118.2 0.0 collective-permute-start.2
  118.2 0.0 copy-done.3
  118.2 4.4 %mul.34 = bf16[16,64,32,64]{3,2,1,0:T(8,128)(2,1)} broadcast(bf16[16,32]{1,0:T(8,128)(2,1)S(1)} %convert_element_type.11), dimensions={0,2} | broadcast | bytes 4195328 | tf_op jit(solution)/shard_map/mul | solution.py:16
  122.6 12.3 %mul.35 = bf16[1024,2048]{1,0:T(8,128)(2,1)} reshape(bf16[16,64,32,64]{3,2,1,0:T(8,128)(2,1)} %mul.34) | data formatting | bytes 8388608 | tf_op jit(solution)/shard_map/mul | solution.py:16
  134.9 7.7 %mul.36 = bf16[1024,2048]{1,0:T(8,128)(2,1)} multiply(bf16[1024,2048]{1,0:T(8,128)(2,1)} %param.4, bf16[1024,2048]{1,0:T(8,128)(2,1)} %mul.35) | non-fusion elementwise | flops 2097152 | bytes 12582912 | tf_op jit(solution)/shard_map/mul | solution.py:16
  142.7 0.0 copy-start
  142.7 0.0 copy-start.2
  142.7 4.8 %broadcast_in_dim.2 = f32[1024,2048]{1,0:T(8,128)} broadcast(f32[]{:T(128)} %constant.36.clone.1), dimensions={} | broadcast | bytes 8388612 | tf_op jit(solution)/shard_map/broadcast_in_dim | solution.py:27
  147.5 0.0 copy-done
  147.5 0.0 copy-done.2
  147.5 3.8 %convolution_dynamic-update-slice_fusion.3 = f32[1024,2048]{1,0:T(8,128)} fusion(f32[1024,2048]{1,0:T(8,128)} %broadcast_in_dim.2, s32[]{:T(128)S(6)} %select_n.32, bf16[1024,2048]{1,0:T(8,128)(2,1)S(1)} %copy-done, bf16[2048,512]{1,0:T(8,128)(2,1)S(1)} %copy-done.2), kind=kOutput, calls=%fused_computation.3 | convolution fusion | flops 2147483648 | bytes 8388612 | tf_op jit(solution)/shard_map/dot_general | solution.py:33
  151.2 3.7 %convolution_dynamic-update-slice_fusion.2 = f32[1024,2048]{1,0:T(8,128)} fusion(f32[1024,2048]{1,0:T(8,128)} %convolution_dynamic-update-slice_fusion.3, s32[]{:T(128)S(6)} %select_n.34, bf16[1024,2048]{1,0:T(8,128)(2,1)S(1)} %copy-done, bf16[2048,512]{1,0:T(8,128)(2,1)S(1)} %collective-permute-done), kind=kOutput, calls=%fused_computation.2 | convolution fusion | flops 2147483648 | bytes 8388612 | tf_op jit(solution)/shard_map/dot_general | solution.py:33
  155.0 5.3 %convolution_dynamic-update-slice_fusion.1 = f32[1024,2048]{1,0:T(8,128)} fusion(f32[1024,2048]{1,0:T(8,128)} %convolution_dynamic-update-slice_fusion.2, s32[]{:T(128)S(6)} %select_n.36, bf16[1024,2048]{1,0:T(8,128)(2,1)S(1)} %copy-done, bf16[2048,512]{1,0:T(8,128)(2,1)} %collective-permute-done.1), kind=kOutput, calls=%fused_computation.1 | convolution fusion | flops 2147483648 | bytes 8388612 | tf_op jit(solution)/shard_map/dot_general | solution.py:33
  160.3 6.0 %collective-permute-done.2 = bf16[2048,512]{1,0:T(8,128)(2,1)} collective-permute-done((bf16[2048,512]{1,0:T(8,128)(2,1)}, bf16[2048,512]{1,0:T(8,128)(2,1)}, u32[]{:S(2)}, u32[]{:S(2)}) %collective-permute-start.2) | collective-permute-done | bytes 2097184 | tf_op jit(solution)/shard_map/ppermute | solution.py:9
  166.2 5.3 %convolution_dynamic-update-slice_fusion = f32[1024,2048]{1,0:T(8,128)} fusion(f32[1024,2048]{1,0:T(8,128)} %convolution_dynamic-update-slice_fusion.1, s32[]{:T(128)S(6)} %select_n.38, bf16[1024,2048]{1,0:T(8,128)(2,1)S(1)} %copy-done, bf16[2048,512]{1,0:T(8,128)(2,1)} %collective-permute-done.2), kind=kOutput, calls=%fused_computation | convolution fusion | flops 2147483648 | bytes 8388612 | tf_op jit(solution)/shard_map/dot_general | solution.py:33
  171.6 0.0 reduce-scatter.2.cloned.1.call-update
  171.6 69.2 %reduce-scatter.2.cloned.1.call-done = f32[1024,256]{1,0:T(8,128)} async-done(((f32[1024,2048]{1,0:T(8,128)}), f32[1024,256]{1,0:T(8,128)}) %reduce-scatter.2.cloned.1.call-update) | async-done | bytes 1048592 | tf_op jit(solution)/shard_map/reduce_scatter | solution.py:35
  240.8 2.1 convert_element_type.13
  (1 shorter events, 0.0 us)
Async XLA Ops:
  6.5 234.2 %reduce-scatter.2.cloned.1.call-start = ((), (), s32[]{:S(2)}) async-start(), calls=%async_computation.1 | async-start | bytes 9437184 | tf_op jit(solution)/shard_map/reduce_scatter | solution.py:35
  15.3 103.0 %copy-start.3 = (s32[16,32]{1,0:T(8,128)S(1)}, s32[16,32]{1,0:T(8,128)}, u32[]{:S(2)}) copy-start(s32[16,32]{1,0:T(8,128)} %param.5) | copy-start | bytes 6148
  17.5 1.3 copy-start.1
  18.8 50.7 %collective-permute-start = (bf16[2048,512]{1,0:T(8,128)(2,1)S(1)}, bf16[2048,512]{1,0:T(8,128)(2,1)S(1)}, u32[]{:S(2)}, u32[]{:S(2)}) collective-permute-start(bf16[2048,512]{1,0:T(8,128)(2,1)S(1)} %mul.39), channel_id=1, source_target_pairs={{0,8},{8,16},{16,24},{24,0},{1,9},{9,17},{17,25},{25,1},{2,10},{10... | collective-permute-start | bytes 6291464 | tf_op jit(solution)/shard_map/ppermute | solution.py:9
  69.5 48.7 %collective-permute-start.1 = (bf16[2048,512]{1,0:T(8,128)(2,1)S(1)}, bf16[2048,512]{1,0:T(8,128)(2,1)}, u32[]{:S(2)}, u32[]{:S(2)}) collective-permute-start(bf16[2048,512]{1,0:T(8,128)(2,1)S(1)} %collective-permute-done), channel_id=1, source_target_pairs={{0,8},{8,16},{16,24},{24,0},{1,9},{9,17},{17,25},{25,1},{2,10},{10... | collective-permute-start | bytes 6291464 | tf_op jit(solution)/shard_map/ppermute | solution.py:9
  118.2 48.0 %collective-permute-start.2 = (bf16[2048,512]{1,0:T(8,128)(2,1)}, bf16[2048,512]{1,0:T(8,128)(2,1)}, u32[]{:S(2)}, u32[]{:S(2)}) collective-permute-start(bf16[2048,512]{1,0:T(8,128)(2,1)} %collective-permute-done.1), channel_id=1, source_target_pairs={{0,8},{8,16},{16,24},{24,0},{1,9},{9,17},{17,25},{25,1},{2,10},{10... | collective-permute-start | bytes 6291464 | tf_op jit(solution)/shard_map/ppermute | solution.py:9
  142.7 4.8 %copy-start = (bf16[1024,2048]{1,0:T(8,128)(2,1)S(1)}, bf16[1024,2048]{1,0:T(8,128)(2,1)}, u32[]{:S(2)}) copy-start(bf16[1024,2048]{1,0:T(8,128)(2,1)} %mul.36) | copy-start | bytes 12582916
  142.7 4.8 %copy-start.2 = (bf16[2048,512]{1,0:T(8,128)(2,1)S(1)}, bf16[2048,512]{1,0:T(8,128)(2,1)}, u32[]{:S(2)}) copy-start(bf16[2048,512]{1,0:T(8,128)(2,1)} %copy-done.1) | copy-start | bytes 6291460
Sparse Core Ops, SparseCore 0:
  171.7 69.0 reduce-scatter.1
where the time goes:
time: 250 us
  waiting for transfers between devices  172 us (69%)
  local copies, waits for them, and re-layouts  30.9 us (12%)
  matrix products  18.1 us (7%)
  between operations  13.4 us (5%)
  other arithmetic  12.7 us (5%)
  starting transfers between devices  3.03 us (1%)
    ppermute x3, waiting for transfers between devices, from_behind(): return lax.ppermute(x, axis, [(i, (i + by) % size) for i in range(size)])  102 us
    reduce_scatter x1, waiting for transfers between devices, local(): lax.psum_scatter(partial_value, ('col', 'layer'), scatter_dimension=1, ti...  69.2 us
    mul x4, local copies, waits for them, and re-layouts, apply_pattern(): masked = shaped * pattern[:, None, :, None].astype(jnp.bfloat16)  24.7 us
    dot_general x4, matrix products, local(): piece = jnp.dot(left, current, preferred_element_type=jnp.float32)  18.1 us
    mul x2, other arithmetic, apply_pattern(): masked = shaped * pattern[:, None, :, None].astype(jnp.bfloat16)  9.9 us
  transfers between devices with their start and end apart: 4, of which 4 were waited for; matrix products, arithmetic and copies ran while one was open for 17% of the time, Pallas kernels for 0%

commit v1 on v0

--- a/solution.py
+++ b/solution.py
@@ -1,7 +1,16 @@
+import functools
+
 import jax
 import jax.numpy as jnp
 from jax import lax
+from jax.experimental import pallas as pl
+from jax.experimental.pallas import tpu as pltpu
 from jax.sharding import PartitionSpec as P
+
+MESH = pl.DeviceIdType.MESH
+BLOCK = 64
+CHUNKS = 4
+CAPS = (160, 256)
 
 
 def from_behind(x, axis, by):
@@ -17,7 +26,7 @@
     return masked.reshape(rows, cols)
 
 
-def local(left_blocks, left_pattern, right_blocks, right_pattern):
+def local_general(left_blocks, left_pattern, right_blocks, right_pattern):
     left = apply_pattern(left_blocks, left_pattern)
     right = apply_pattern(right_blocks, right_pattern)
     left_rows = left.shape[0]
@@ -36,6 +45,297 @@
     return reduced.astype(jnp.bfloat16)
 
 
+def turn(tile):
+    return jnp.concatenate([tile[:, BLOCK:], tile[:, :BLOCK]], axis=1)
+
+
+def join(a, b, stay_a, turn_a, stay_b, turn_b):
+    left = jnp.where(lax.broadcasted_iota(jnp.int32, (1, 128), 1) < BLOCK, 1.0, 0.0)
+    right = 1.0 - left
+    first = a * (left * stay_a).astype(jnp.bfloat16) + turn(a) * (left * turn_a).astype(jnp.bfloat16)
+    second = b * (right * stay_b).astype(jnp.bfloat16) + turn(b) * (right * turn_b).astype(jnp.bfloat16)
+    return first + second
+
+
+def kernel(cap, left_ref, lpat_ref, right_ref, tile_ref, stay_ref, turn_ref, from_ref, keep_ref, flip_ref, out_ref,
+           masked, tiled, held, current, wide, part, swapped, got, done,
+           zsend, zrecv, xsend, xrecv, rsend, rrecv, fsend, frecv):
+    z = lax.axis_index("row")
+    col = lax.axis_index("col")
+    layer = lax.axis_index("layer")
+    core = lax.rem(layer, 2)
+    chip = col * 2 + lax.div(layer, 2)
+    tiles = cap // 2 // CHUNKS
+    rows, width = left_ref.shape[0], right_ref.shape[1]
+    quarter = rows // 4
+    half = width // 2
+    kblocks = right_ref.shape[0] // BLOCK
+    strips = width // 128
+
+    def at_chip(q):
+        return (z, lax.div(q, 2), lax.rem(q, 2) * 2 + core)
+
+    partner = (z, col, lax.div(layer, 2) * 2 + 1 - core)
+    above, below = (z + 1, col, layer), (z - 1, col, layer)
+    has_above, has_below = z < 3, z > 0
+
+    barrier = pltpu.get_barrier_semaphore()
+
+    @pl.when(has_above)
+    def _():
+        pl.semaphore_signal(barrier, inc=1, device_id=above, device_id_type=MESH)
+
+    @pl.when(has_below)
+    def _():
+        pl.semaphore_signal(barrier, inc=1, device_id=below, device_id_type=MESH)
+
+    pl.semaphore_signal(barrier, inc=1, device_id=partner, device_id_type=MESH)
+    for i in range(1, 4):
+        pl.semaphore_signal(barrier, inc=1, device_id=at_chip(lax.rem(chip + i, 4)), device_id_type=MESH)
+    pl.semaphore_wait(barrier, 4 + jnp.where(has_above, 1, 0) + jnp.where(has_below, 1, 0))
+
+    def up(j, c):
+        piece = held.at[j, pl.ds(c * tiles, tiles)]
+        return pltpu.make_async_remote_copy(
+            src_ref=piece, dst_ref=piece, send_sem=zsend.at[0, j, c], recv_sem=zrecv.at[j, c],
+            device_id=above, device_id_type=MESH)
+
+    def down(j, c):
+        piece = held.at[j, pl.ds(c * tiles, tiles)]
+        return pltpu.make_async_remote_copy(
+            src_ref=piece, dst_ref=piece, send_sem=zsend.at[1, j, c], recv_sem=zrecv.at[j, c],
+            device_id=below, device_id_type=MESH)
+
+    def pack(c):
+        def one(t, carry):
+            e, o = 2 * t, 2 * t + 1
+            held[z, t] = join(tiled[from_ref[e]], tiled[from_ref[o]],
+                              keep_ref[e], flip_ref[e], keep_ref[o], flip_ref[o])
+            return carry
+        lax.fori_loop(c * tiles, (c + 1) * tiles, one, 0)
+
+    def cut(k, carry):
+        for m in range(strips):
+            tiled[k * strips + m] = right_ref[pl.ds(pl.multiple_of(k * BLOCK, BLOCK), BLOCK), m * 128:(m + 1) * 128]
+        return carry
+
+    lax.fori_loop(0, kblocks, cut, 0)
+    for c in range(CHUNKS):
+        pack(c)
+
+        @pl.when(has_above)
+        def _():
+            up(z, c).start()
+
+        @pl.when(has_below)
+        def _():
+            down(z, c).start()
+
+    depth = left_ref.shape[1]
+    spread = (lax.broadcasted_iota(jnp.int32, (depth // BLOCK, depth), 1) // BLOCK
+              == lax.broadcasted_iota(jnp.int32, (depth // BLOCK, depth), 0))
+    lmask = jnp.dot(lpat_ref[...].astype(jnp.float32), jnp.where(spread, 1.0, 0.0),
+                    preferred_element_type=jnp.float32)
+    for i in range(rows // BLOCK):
+        masked[i * BLOCK:(i + 1) * BLOCK, :] = (
+            left_ref[i * BLOCK:(i + 1) * BLOCK, :] * lmask[i:i + 1, :].astype(jnp.bfloat16))
+
+    def order(r):
+        if r == 0:
+            return z
+        y = jnp.where(z < 2, z, 3 - z)
+        o = {1: y + 1, 2: 2 - 2 * y, 3: 3 + 0 * y}[r]
+        return jnp.where(z < 2, o, 3 - o)
+
+    def step(t):
+        away, c = t // CHUNKS + 1, t % CHUNKS
+
+        @pl.when(z + away <= 3)
+        def _():
+            j = z + away
+            down(j, c).wait_recv()
+
+            @pl.when(has_below)
+            def _():
+                down(j, c).start()
+
+        @pl.when(z - away >= 0)
+        def _():
+            j = z - away
+            up(j, c).wait_recv()
+
+            @pl.when(has_above)
+            def _():
+                up(j, c).start()
+
+    def expand(r):
+        j = order(r)
+
+        def fetch(t, carry):
+            current[t] = held[j, t]
+            return carry
+        lax.fori_loop(0, cap // 2, fetch, 0)
+
+        def one(k, carry):
+            for m in range(strips):
+                e = (j * kblocks + k) * (2 * strips) + 2 * m
+                o = e + 1
+                wide[pl.ds(pl.multiple_of(k * BLOCK, BLOCK), BLOCK), m * 128:(m + 1) * 128] = join(
+                    current[tile_ref[e]], current[tile_ref[o]],
+                    stay_ref[e], turn_ref[e], stay_ref[o], turn_ref[o])
+            return carry
+        lax.fori_loop(0, kblocks, one, 0)
+
+    def swap(r, q):
+        return pltpu.make_async_remote_copy(
+            src_ref=part.at[r, 1 - core, q], dst_ref=swapped.at[r, q],
+            send_sem=xsend.at[r, q], recv_sem=xrecv.at[r, q],
+            device_id=partner, device_id_type=MESH)
+
+    def multiply(r):
+        def one(i, carry):
+            q = lax.rem(chip + 1 + i, 4)
+            piece = jnp.dot(masked[pl.ds(pl.multiple_of(q * quarter, quarter), quarter), :], wide[...],
+                            preferred_element_type=jnp.float32)
+            part[r, 0, q] = piece[:, :half]
+            part[r, 1, q] = piece[:, half:]
+            swap(r, q).start()
+            return carry
+        lax.fori_loop(0, 4, one, 0)
+
+    def scatter(r, i):
+        q = lax.rem(chip + i, 4)
+        return pltpu.make_async_remote_copy(
+            src_ref=part.at[r, core, q], dst_ref=got.at[r, 3 - i],
+            send_sem=rsend.at[r, i - 1], recv_sem=rrecv.at[r, 3 - i],
+            device_id=at_chip(q), device_id_type=MESH)
+
+    def arrival(r, i):
+        return pltpu.make_async_remote_copy(
+            src_ref=part.at[r, core, chip], dst_ref=got.at[r, i - 1],
+            send_sem=rsend.at[r, i - 1], recv_sem=rrecv.at[r, i - 1],
+            device_id=at_chip(lax.rem(chip + i, 4)), device_id_type=MESH)
+
+    def add_cores(r):
+        for i in range(1, 5):
+            q = lax.rem(chip + i, 4)
+            swap(r, q).wait_recv()
+            part[r, core, q] = part[r, core, q] + swapped[r, q]
+            if i < 4:
+                scatter(r, i).start()
+
+    def finish(r):
+        j = order(r)
+        mine = pl.ds(pl.multiple_of(chip * quarter, quarter), quarter)
+        for i in range(1, 4):
+            arrival(r, i).wait_recv()
+        total = (part[r, core, chip] + got[r, 0]) + (got[r, 1] + got[r, 2])
+
+        @pl.when(j == chip)
+        def _():
+            out_ref[mine, :] = total.astype(jnp.bfloat16)
+
+        @pl.when(j != chip)
+        def _():
+            done[r] = total.astype(jnp.bfloat16)
+            deliver(r, j, chip).start()
+
+    def deliver(r, to, source):
+        rng = pl.ds(pl.multiple_of(source * quarter, quarter), quarter)
+        return pltpu.make_async_remote_copy(
+            src_ref=done.at[r], dst_ref=out_ref.at[rng], send_sem=fsend.at[r], recv_sem=frecv.at[source],
+            device_id=at_chip(to), device_id_type=MESH)
+
+    for r in range(4):
+        if r > 0:
+            step((r - 1) * CHUNKS + CHUNKS - 1)
+        expand(r)
+        if r < 3:
+            step(r * CHUNKS)
+        multiply(r)
+        if r < 3:
+            step(r * CHUNKS + 1)
+        add_cores(r)
+        if r < 3:
+            step(r * CHUNKS + 2)
+        finish(r)
+
+    for i in range(1, 4):
+        q = lax.rem(chip + i, 4)
+        deliver(0, q, q).wait_recv()
+    for r in range(4):
+        @pl.when(order(r) != chip)
+        def _():
+            deliver(r, order(r), chip).wait_send()
+        for q in range(4):
+            swap(r, q).wait_send()
+        for i in range(1, 4):
+            scatter(r, i).wait_send()
+    for j in range(4):
+        for c in range(CHUNKS):
+            @pl.when(has_above & (j <= z))
+            def _():
+                up(j, c).wait_send()
+
+            @pl.when(has_below & (j >= z))
+            def _():
+                down(j, c).wait_send()
+
+
+def run(cap, index, left, lpat, right, present, slot, inv):
+    rows, width = left.shape[0], right.shape[1]
+    quarter, half = rows // 4, width // 2
+    dma = pltpu.SemaphoreType.DMA
+    vmem = pl.BlockSpec(memory_space=pltpu.VMEM)
+    smem = pl.BlockSpec(memory_space=pltpu.SMEM)
+    side = jnp.arange(slot.size, dtype=jnp.int32) % 2
+    same = (slot % 2 == side).astype(jnp.float32)
+    there = present.astype(jnp.float32)
+    tile = jnp.minimum(slot // 2, cap // 2 - 1)
+    keep = (inv % 2 == jnp.arange(inv.size, dtype=jnp.int32) % 2).astype(jnp.float32)
+    tiles = (right.shape[0] // BLOCK) * (width // 128)
+    return pl.pallas_call(
+        functools.partial(kernel, cap),
+        out_shape=jax.ShapeDtypeStruct((rows, half), jnp.bfloat16),
+        in_specs=[vmem, vmem, vmem] + [smem] * 6,
+        out_specs=vmem,
+        scratch_shapes=[
+            pltpu.VMEM(left.shape, jnp.bfloat16),
+            pltpu.VMEM((tiles, BLOCK, 128), jnp.bfloat16),
+            pltpu.VMEM((4, cap // 2, BLOCK, 128), jnp.bfloat16),
+            pltpu.VMEM((cap // 2, BLOCK, 128), jnp.bfloat16),
+            pltpu.VMEM(right.shape, jnp.bfloat16),
+            pltpu.VMEM((4, 2, 4, quarter, half), jnp.float32),
+            pltpu.VMEM((4, 4, quarter, half), jnp.float32),
+            pltpu.VMEM((4, 3, quarter, half), jnp.float32),
+            pltpu.VMEM((4, quarter, half), jnp.bfloat16),
+            dma((2, 4, CHUNKS)), dma((4, CHUNKS)),
+            dma((4, 4)), dma((4, 4)), dma((4, 3)), dma((4, 3)), dma((4,)), dma((4,)),
+        ],
+        compiler_params=pltpu.CompilerParams(
+            collective_id=index, has_side_effects=True, vmem_limit_bytes=56 * 2**20),
+        name=f"sparse_product_{cap}",
+    )(left, lpat, right, tile, there * same, there * (1 - same), inv // 2, keep, 1 - keep)
+
+
+def local_packed(left, lpat, right, rpat):
+    every = lax.all_gather(rpat, ("layer", "col", "row"), axis=0, tiled=False)
+    everyone = every.reshape(-1, 4, rpat.size)
+    most = jnp.max(jnp.sum(everyone, axis=2))
+    group = lax.axis_index("layer") * lax.axis_size("col") + lax.axis_index("col")
+    present = lax.dynamic_index_in_dim(everyone, group, 0, keepdims=False)
+    slot = jnp.cumsum(present, axis=1) - present
+    own = rpat.reshape(-1)
+    place = jnp.cumsum(own) - own
+    index = jnp.arange(own.size, dtype=jnp.int32)
+    hit = (place[None, :] == index[:, None]) & (own[None, :] > 0)
+    inv = jnp.sum(jnp.where(hit, index[None, :], 0), axis=1)
+    which = sum((most > cap).astype(jnp.int32) for cap in CAPS[:-1])
+    return lax.switch(
+        which, [functools.partial(run, cap, i) for i, cap in enumerate(CAPS)],
+        left, lpat, right, present.reshape(-1), slot.reshape(-1), inv)
+
+
 def solution(mesh):
     placed = (
         P("row", ("layer", "col")),
@@ -43,6 +343,8 @@
         P(("layer", "col"), "row"),
         P(("layer", "col"), "row"),
     )
+    sizes = tuple(mesh.shape[axis] for axis in ("row", "col", "layer"))
+    local = local_packed if sizes == (4, 2, 4) else local_general
     return jax.shard_map(
         local, mesh=mesh, in_specs=placed, out_specs=P("row", ("col", "layer")), check_vma=False
     )

time: 250 us -> 196 us (0.78)
  waiting for transfers between devices: 172 us -> 0 us
  Pallas kernels: 0 us -> 113 us
  blocking collectives: 0 us -> 71 us
  local copies, waits for them, and re-layouts: 30.9 us -> 2.75 us
  matrix products: 18.1 us -> 0 us
  between operations: 13.4 us -> 0.71 us
  other arithmetic: 12.7 us -> 6.16 us
  starting transfers between devices: 3.03 us -> 0 us
    pallas_call x0 -> x1, Pallas kernels: none -> 113 us  [run(): pl.pallas_call(functools.partial(kernel, cap), out_shape=jax.ShapeDtypeSt...]
    ppermute x3 -> x0, waiting for transfers between devices: 102 us -> none  [from_behind(): return lax.ppermute(x, axis, [(i, (i + by) % size) for i in range(size)])]
    all_gather x0 -> x1, blocking collectives: none -> 71 us  [local_packed(): every = lax.all_gather(rpat, ('layer', 'col', 'row'), axis=0, tiled=False)]
    reduce_scatter x1 -> x0, waiting for transfers between devices: 69.2 us -> none  [local(): lax.psum_scatter(partial_value, ('col', 'layer'), scatter_dimension=1, ti...]
    mul x4 -> x0, local copies, waits for them, and re-layouts: 24.7 us -> none  [apply_pattern(): masked = shaped * pattern[:, None, :, None].astype(jnp.bfloat16)]
    dot_general x4 -> x0, matrix products: 18.1 us -> none  [local(): piece = jnp.dot(left, current, preferred_element_type=jnp.float32)]
    mul x2, other arithmetic: 9.9 us -> 1.19 us  [the longest x1 0.61 us: run(): there * (1 - same)]
    broadcast_in_dim x1, local copies, waits for them, and re-layouts: 4.8 us -> 0.02 us  [local_packed(): inv = jnp.sum(jnp.where(hit, index[None, :], 0), axis=1)]
  transfers between devices with their start and end apart: 4 -> 0, of which waited for: 4 -> 0; matrix products, arithmetic and copies ran while one was open for 17% -> 0% of each run, Pallas kernels for 0% -> 0%
where the time goes in v1:
time: 196 us; the launch traced here: 193 us
  Pallas kernels  113 us (58%)
  blocking collectives  71 us (36%)
  other arithmetic  6.16 us (3%)
  local copies, waits for them, and re-layouts  2.75 us (1%)
    pallas_call x1, Pallas kernels, run(): pl.pallas_call(functools.partial(kernel, cap), out_shape=jax.ShapeDtypeSt...  113 us
    all_gather x1, blocking collectives, local_packed(): every = lax.all_gather(rpat, ('layer', 'col', 'row'), axis=0, tiled=False)  71 us

profile of v1, /device:TPU:0, one launch (start us, length us, event | category | flops | bytes accessed | tf_op | source)
XLA Modules:
  0.0 193.3 jit_solution(5228788067029809401)
XLA Ops:
  0.0 0.8 copy.35
  0.8 0.1 reshape.65
  0.9 0.1 reshape.63
  0.9 0.3 reduce-window.19
  1.2 0.1 slice.15
  1.4 71.0 %all-gather.1 = s32[32,32,8]{1,2,0:T(8,128)S(1)} all-gather(s32[1,32,8]{1,2,0:T(8,128)} %bitcast.23), channel_id=2, replica_groups=mesh['row'=4,'col'=2,'layer'=4] {'layer','col','row'}, dimensions={0}, use_global_device_ids=true | all-gather | bytes 33792 | tf_op jit(solution)/shard_map/all_gather | solution.py:322
  72.3 0.7 reduce_sum.18
  73.0 0.6 reduce_max.9
  74.3 0.2 copy.34
  74.6 0.3 reshape.60
  74.9 1.2 reduce-window.15
  76.1 0.1 slice.25
  76.2 0.1 copy.36
  76.3 116.2 %conditional.1 = (bf16[1024,256]{1,0:T(8,128)(2,1)S(1)}) conditional(s32[]{:T(128)} %clamp.3, (s32[4,2,128]{2,1,0:T(2,128)S(1)}, s32[1024]{0:T(1024)S(1)}, s32[2,128]{1,0:T(2,128)S(1)}, bf16[1024,2048]{1,0:T(8,128)(2,1)}, s32[16,32]{1,0:T(8,128)}, /*index=5*/bf16[2048,512]{1,0:T(8,128)(2,1)}, s32[]{:T(128)}, s32[256,256]{1,0:T(8,128)S(1)}, ...), branch_computations={%region_7.8_spmd.clone, %region_8.9_spmd.clone} | conditional | flops 315648 | bytes 579268 | solution.py:334
  76.3 0.1 copy.39
  76.4 0.1 bitcast_subtract_fusion
  76.5 0.1 select_reduce_fusion
  76.7 0.6 and_select_fusion.2.from_ref
  77.2 0.6 broadcast_subtract_fusion
  77.8 0.1 copy.38
  77.9 0.1 broadcast_add_fusion
  78.0 0.6 fusion.tile_ref
  78.6 0.6 subtract_multiply_fusion
  79.2 0.6 convert_select_fusion.stay_ref
  79.8 112.7 %sparse_product_160.1 = bf16[1024,256]{1,0:T(8,128)(2,1)S(1)} custom-call(bf16[1024,2048]{1,0:T(8,128)(2,1)} %get-tuple-element.121.left_ref, s32[16,32]{1,0:T(8,128)} %get-tuple-element.122.lpat_ref, bf16[2048,512]{1,0:T(8,128)(2,1)} %get-tuple-element.123.right_ref, s32[1024]{0:T(1024)} %fusion.tile_ref, f32[1024]{0:T(1024)} %convert_select_fusion.stay_ref, ...), custom_call_target="tpu_custom_call" | custom-call | tf_op jit(solution)/shard_map/cond/branch_0_fun/sparse_product_160/pallas_call | solution.py:297
  192.5 0.8 copy.46
  (10 shorter events, 0.2 us)

commit v2 on v0

--- a/solution.py
+++ b/solution.py
@@ -1,7 +1,17 @@
+import functools
+
 import jax
 import jax.numpy as jnp
 from jax import lax
+from jax.experimental import pallas as pl
+from jax.experimental.pallas import tpu as pltpu
 from jax.sharding import PartitionSpec as P
+
+MESH = pl.DeviceIdType.MESH
+BLOCK = 64
+CAP = 160
+CHUNKS = 8
+READY = (3, 5, 7, 8)
 
 
 def from_behind(x, axis, by):
@@ -17,7 +27,7 @@
     return masked.reshape(rows, cols)
 
 
-def local(left_blocks, left_pattern, right_blocks, right_pattern):
+def local_general(left_blocks, left_pattern, right_blocks, right_pattern):
     left = apply_pattern(left_blocks, left_pattern)
     right = apply_pattern(right_blocks, right_pattern)
     left_rows = left.shape[0]
@@ -36,6 +46,346 @@
     return reduced.astype(jnp.bfloat16)
 
 
+def turn(tile):
+    return jnp.concatenate([tile[:, BLOCK:], tile[:, :BLOCK]], axis=1)
+
+
+def join(a, b, stay_a, turn_a, stay_b, turn_b):
+    left = jnp.where(lax.broadcasted_iota(jnp.int32, (1, 128), 1) < BLOCK, 1.0, 0.0)
+    right = 1.0 - left
+    first = a * (left * stay_a).astype(jnp.bfloat16) + turn(a) * (left * turn_a).astype(jnp.bfloat16)
+    second = b * (right * stay_b).astype(jnp.bfloat16) + turn(b) * (right * turn_b).astype(jnp.bfloat16)
+    return first + second
+
+
+def kernel(left_ref, lpat_ref, right_ref, code_ref, pack_ref, out_ref, flag_ref,
+           masked, tiled, held, current, wide, part, swapped, got, done, codes, scalars, flags,
+           zsend, zrecv, xsend, xrecv, rsend, rrecv, fsend, frecv, csend, crecv, ssem, gsend, grecv):
+    z = lax.axis_index("row")
+    col = lax.axis_index("col")
+    layer = lax.axis_index("layer")
+    core = lax.rem(layer, 2)
+    chip = col * 2 + lax.div(layer, 2)
+    tiles = CAP // 2 // CHUNKS
+    rows = left_ref.shape[0]
+    quarter, eighth = rows // 4, rows // 8
+    kblocks = right_ref.shape[0] // BLOCK
+    strips = right_ref.shape[1] // 128
+
+    def device(q, which):
+        return (z, lax.div(q, 2), lax.rem(q, 2) * 2 + which)
+
+    def other(i):
+        return lax.rem(chip + i, 4)
+
+    def on_line(i):
+        return (lax.rem(z + i, 4), col, layer)
+
+    partner = device(chip, 1 - core)
+    above, below = (z + 1, col, layer), (z - 1, col, layer)
+    has_above, has_below = z < 3, z > 0
+
+    def remote(src, dst, send, recv, to):
+        return pltpu.make_async_remote_copy(
+            src_ref=src, dst_ref=dst, send_sem=send, recv_sem=recv, device_id=to, device_id_type=MESH)
+
+    barrier = pltpu.get_barrier_semaphore()
+    for to in [partner] + [on_line(i) for i in (1, 2, 3)] + [device(other(i), core) for i in (1, 2, 3)]:
+        pl.semaphore_signal(barrier, inc=1, device_id=to, device_id_type=MESH)
+    codes[z] = code_ref[...]
+
+    def cut(k, carry):
+        for m in range(strips):
+            tiled[m * kblocks + k] = right_ref[pl.ds(pl.multiple_of(k * BLOCK, BLOCK), BLOCK), m * 128:(m + 1) * 128]
+        return carry
+
+    lax.fori_loop(0, kblocks, cut, 0)
+
+    def pack(c):
+        def one(t, carry):
+            row, e = lax.div(t, 64), lax.rem(t, 64) * 2
+            held[z, t] = join(
+                tiled[pack_ref[row, e]], tiled[pack_ref[row, e + 1]],
+                pack_ref[2 + row, e].astype(jnp.float32), pack_ref[4 + row, e].astype(jnp.float32),
+                pack_ref[2 + row, e + 1].astype(jnp.float32), pack_ref[4 + row, e + 1].astype(jnp.float32))
+            return carry
+        lax.fori_loop(c * tiles, (c + 1) * tiles, one, 0)
+
+    def up(j, c):
+        piece = held.at[j, pl.ds(c * tiles, tiles)]
+        return remote(piece, piece, zsend.at[0, j, c], zrecv.at[j, c], above)
+
+    def down(j, c):
+        piece = held.at[j, pl.ds(c * tiles, tiles)]
+        return remote(piece, piece, zsend.at[1, j, c], zrecv.at[j, c], below)
+
+    def tell(i):
+        return remote(codes.at[z], codes.at[z], csend.at[i - 1], crecv.at[z], on_line(i))
+
+    def told(i):
+        j = lax.rem(z + i, 4)
+        return remote(codes.at[j], codes.at[j], csend.at[i - 1], crecv.at[j], on_line(i))
+
+    pack(0)
+    pl.semaphore_wait(barrier, 7)
+    for i in range(1, 4):
+        tell(i).start()
+    for c in range(CHUNKS):
+        if c > 0:
+            pack(c)
+
+        @pl.when(has_above)
+        def _():
+            up(z, c).start()
+
+        @pl.when(has_below)
+        def _():
+            down(z, c).start()
+
+    depth = left_ref.shape[1]
+    spread = (lax.broadcasted_iota(jnp.int32, (depth // BLOCK, depth), 1) // BLOCK
+              == lax.broadcasted_iota(jnp.int32, (depth // BLOCK, depth), 0))
+    lmask = jnp.dot(lpat_ref[...].astype(jnp.float32), jnp.where(spread, 1.0, 0.0),
+                    preferred_element_type=jnp.float32)
+    for i in range(rows // BLOCK):
+        masked[i * BLOCK:(i + 1) * BLOCK, :] = (
+            left_ref[i * BLOCK:(i + 1) * BLOCK, :] * lmask[i:i + 1, :].astype(jnp.bfloat16))
+
+    for i in range(1, 4):
+        told(i).wait_recv()
+    to_scalars = pltpu.make_async_copy(codes, scalars, ssem)
+    to_scalars.start()
+    to_scalars.wait()
+    flags[0] = jnp.maximum(jnp.maximum(codes[0], codes[1]), jnp.maximum(codes[2], codes[3]))
+    pair = remote(flags.at[0], flags.at[1], gsend.at[0], grecv.at[0], partner)
+    pair.start()
+
+    def spread_flag(i):
+        return remote(flags.at[2], flags.at[6 - i], gsend.at[i], grecv.at[4 - i], device(other(i), core))
+
+    def flag_from(i):
+        return remote(flags.at[2], flags.at[2 + i], gsend.at[i], grecv.at[i], device(other(i), core))
+
+    def order(r):
+        y = jnp.where(z < 2, z, 3 - z)
+        o = jnp.where(r == 0, y, jnp.where(r == 1, y + 1, jnp.where(r == 2, 2 - 2 * y, 3)))
+        return jnp.where(z < 2, o, 3 - o)
+
+    def step(r, c):
+        @pl.when((r > 0) & (z + r <= 3))
+        def _():
+            j = z + r
+            down(j, c).wait_recv()
+
+            @pl.when(has_below)
+            def _():
+                down(j, c).start()
+
+        @pl.when((r > 0) & (z - r >= 0))
+        def _():
+            j = z - r
+            up(j, c).wait_recv()
+
+            @pl.when(has_above)
+            def _():
+                up(j, c).start()
+
+    def expand(r, g):
+        j = order(r)
+
+        def fetch(t, carry):
+            current[t] = held[j, t]
+            return carry
+        first = 0 if g == 0 else READY[g - 1]
+        lax.fori_loop(first * tiles, READY[g] * tiles, fetch, 0)
+
+        def one(k, carry):
+            row, e = g // 2, (g % 2) * 64 + 2 * k
+            wide[pl.ds(pl.multiple_of(k * BLOCK, BLOCK), BLOCK), :] = join(
+                current[scalars[j, row, e]], current[scalars[j, row, e + 1]],
+                scalars[j, 2 + row, e].astype(jnp.float32), scalars[j, 4 + row, e].astype(jnp.float32),
+                scalars[j, 2 + row, e + 1].astype(jnp.float32), scalars[j, 4 + row, e + 1].astype(jnp.float32))
+            return carry
+        lax.fori_loop(0, kblocks, one, 0, unroll=4)
+
+    def swap(n, q):
+        return remote(part.at[n, q, 1 - core], swapped.at[n, q], xsend.at[n, q], xrecv.at[n, q], partner)
+
+    def multiply(n):
+        def one(i, carry):
+            q = lax.rem(chip + 1 + i, 4)
+            piece = jnp.dot(masked[pl.ds(pl.multiple_of(q * quarter, quarter), quarter), :], wide[...],
+                            preferred_element_type=jnp.float32)
+            part[n, q, 0] = piece[:eighth]
+            part[n, q, 1] = piece[eighth:]
+            swap(n, q).start()
+            return carry
+        lax.fori_loop(0, 4, one, 0)
+
+    def scatter(n, i):
+        return remote(part.at[n, other(i), core], got.at[n, 3 - i], rsend.at[n, i - 1], rrecv.at[n, 3 - i],
+                      device(other(i), core))
+
+    def arrival(n, i):
+        return remote(part.at[n, chip, core], got.at[n, i - 1], rsend.at[n, i - 1], rrecv.at[n, i - 1],
+                      device(other(i), core))
+
+    def add_cores(n):
+        for i in range(1, 5):
+            q = other(i)
+            swap(n, q).wait_recv()
+            part[n, q, core] = part[n, q, core] + swapped[n, q]
+            if i < 4:
+                scatter(n, i).start()
+
+    def deliver(n, to, which, place, source, source_core):
+        rng = pl.ds(pl.multiple_of(source * quarter + source_core * eighth, eighth), eighth)
+        return remote(done.at[n], out_ref.at[rng, pl.ds(pl.multiple_of(place * 128, 128), 128)],
+                      fsend.at[n], frecv.at[place, source, source_core], device(to, which))
+
+    def finish(n, r, g):
+        j, which, place = order(r), g // 2, g % 2
+        for i in range(1, 4):
+            arrival(n, i).wait_recv()
+        total = (part[n, chip, core] + got[n, 0]) + (got[n, 1] + got[n, 2])
+        here = (j == chip) & (core == which)
+
+        @pl.when(here)
+        def _():
+            rng = pl.ds(pl.multiple_of(chip * quarter + core * eighth, eighth), eighth)
+            out_ref[rng, place * 128:(place + 1) * 128] = total.astype(jnp.bfloat16)
+
+        @pl.when(jnp.logical_not(here))
+        def _():
+            done[n] = total.astype(jnp.bfloat16)
+            deliver(n, j, which, place, chip, core).start()
+
+    def rank(r, carry):
+        for g in range(strips):
+            n = r * strips + g
+            for c in range(0 if g == 0 else READY[g - 1], READY[g]):
+                step(r, c)
+            expand(r, g)
+            multiply(n)
+            add_cores(n)
+            if g > 0:
+                finish(n - 1, r, g - 1)
+            else:
+                @pl.when(r > 0)
+                def _():
+                    finish(n - 1, r - 1, strips - 1)
+        return carry
+
+    pair.wait_recv()
+    flags[2] = jnp.maximum(flags[0], flags[1])
+    for i in range(1, 4):
+        spread_flag(i).start()
+    lax.fori_loop(0, 4, rank, 0)
+    finish(4 * strips - 1, 3, strips - 1)
+
+    for i in range(1, 4):
+        flag_from(i).wait_recv()
+    flag_ref[...] = jnp.maximum(jnp.maximum(flags[2], flags[3]), jnp.maximum(flags[4], flags[5]))
+    pair.wait_send()
+    for i in range(1, 4):
+        spread_flag(i).wait_send()
+        tell(i).wait_send()
+
+    for place in range(2):
+        for i in range(4):
+            for source_core in range(2):
+                @pl.when((i > 0) | (core != source_core))
+                def _():
+                    deliver(0, chip, core, place, other(i), source_core).wait_recv()
+
+    def drain(r, carry):
+        for g in range(strips):
+            n = r * strips + g
+
+            @pl.when((order(r) != chip) | (core != g // 2))
+            def _():
+                deliver(n, order(r), g // 2, g % 2, chip, core).wait_send()
+            for q in range(4):
+                swap(n, q).wait_send()
+            for i in range(1, 4):
+                scatter(n, i).wait_send()
+        for c in range(CHUNKS):
+            @pl.when(has_above & (r <= z))
+            def _():
+                up(r, c).wait_send()
+
+            @pl.when(has_below & (r >= z))
+            def _():
+                down(r, c).wait_send()
+        return carry
+
+    lax.fori_loop(0, 4, drain, 0)
+
+
+def run(left, lpat, right, code, pack):
+    rows, width = left.shape[0], right.shape[1]
+    eighth = rows // 8
+    strips = width // 128
+    units = 4 * strips
+    dma = pltpu.SemaphoreType.DMA
+    vmem = pl.BlockSpec(memory_space=pltpu.VMEM)
+    smem = pl.BlockSpec(memory_space=pltpu.SMEM)
+    tiles = (right.shape[0] // BLOCK) * strips
+    return pl.pallas_call(
+        kernel,
+        out_shape=(jax.ShapeDtypeStruct((rows, width // 2), jnp.bfloat16),
+                   jax.ShapeDtypeStruct((8, 128), jnp.int32)),
+        in_specs=[vmem, vmem, vmem, vmem, smem],
+        out_specs=(vmem, vmem),
+        scratch_shapes=[
+            pltpu.VMEM(left.shape, jnp.bfloat16),
+            pltpu.VMEM((tiles, BLOCK, 128), jnp.bfloat16),
+            pltpu.VMEM((4, CAP // 2, BLOCK, 128), jnp.bfloat16),
+            pltpu.VMEM((CAP // 2, BLOCK, 128), jnp.bfloat16),
+            pltpu.VMEM((right.shape[0], 128), jnp.bfloat16),
+            pltpu.VMEM((units, 4, 2, eighth, 128), jnp.float32),
+            pltpu.VMEM((units, 4, eighth, 128), jnp.float32),
+            pltpu.VMEM((units, 3, eighth, 128), jnp.float32),
+            pltpu.VMEM((units, eighth, 128), jnp.bfloat16),
+            pltpu.VMEM((4, 8, 128), jnp.int32),
+            pltpu.SMEM((4, 8, 128), jnp.int32),
+            pltpu.VMEM((6, 8, 128), jnp.int32),
+            dma((2, 4, CHUNKS)), dma((4, CHUNKS)),
+            dma((units, 4)), dma((units, 4)), dma((units, 3)), dma((units, 3)),
+            dma((units,)), dma((2, 4, 2)), dma((3,)), dma((4,)), dma, dma((4,)), dma((4,)),
+        ],
+        compiler_params=pltpu.CompilerParams(
+            collective_id=0, has_side_effects=True, vmem_limit_bytes=56 * 2**20),
+        name="sparse_product",
+    )(left, lpat, right, code, pack)
+
+
+def local_packed(left, lpat, right, rpat):
+    kblocks, cols = rpat.shape
+    present = rpat.reshape(kblocks, cols // 2, 2).transpose(1, 0, 2).reshape(-1)
+    count = present.size
+    upto = jnp.cumsum(present)
+    slot = upto - present
+    index = jnp.arange(count, dtype=jnp.int32)
+    there = present > 0
+    same = (slot - index) % 2 == 0
+    ends = upto.reshape(cols // 2, -1)[:, -1]
+    room = jnp.array([ready * (CAP // CHUNKS) for ready in READY], jnp.int32)
+    over = jnp.any(ends > room).astype(jnp.int32)
+    code = jnp.stack([
+        jnp.where(there, jnp.minimum(slot // 2, CAP // 2 - 1), 0),
+        (there & same).astype(jnp.int32),
+        (there & jnp.logical_not(same)).astype(jnp.int32),
+        jnp.broadcast_to(over, (count,)),
+    ]).reshape(8, 128)
+    hit = (slot[None, :] == index[:, None]) & there[None, :]
+    source = jnp.sum(jnp.where(hit, index[None, :], 0), axis=1)
+    keep = ((source - index) % 2 == 0).astype(jnp.int32)
+    pack = jnp.stack([source // 2, keep, 1 - keep]).reshape(6, 128)
+    out, flag = run(left, lpat, right, code, pack)
+    return lax.cond(flag[6, 0] > 0, local_general, lambda *_: out, left, lpat, right, rpat)
+
+
 def solution(mesh):
     placed = (
         P("row", ("layer", "col")),
@@ -43,6 +393,8 @@
         P(("layer", "col"), "row"),
         P(("layer", "col"), "row"),
     )
+    sizes = tuple(mesh.shape[axis] for axis in ("row", "col", "layer"))
+    local = local_packed if sizes == (4, 2, 4) else local_general
     return jax.shard_map(
         local, mesh=mesh, in_specs=placed, out_specs=P("row", ("col", "layer")), check_vma=False
     )

time: 250 us -> 131 us (0.52)
  waiting for transfers between devices: 172 us -> 0 us
  Pallas kernels: 0 us -> 108 us
  local copies, waits for them, and re-layouts: 30.9 us -> 5.05 us
  matrix products: 18.1 us -> 0 us
  other arithmetic: 12.7 us -> 2.16 us
  starting transfers between devices: 3.03 us -> 0 us
    pallas_call x0 -> x1, Pallas kernels: none -> 108 us  [run(): pl.pallas_call(kernel, out_shape=(jax.ShapeDtypeStruct((rows, width // 2)...]
    ppermute x3 -> x0, waiting for transfers between devices: 102 us -> none  [from_behind(): return lax.ppermute(x, axis, [(i, (i + by) % size) for i in range(size)])]
    reduce_scatter x1 -> x0, waiting for transfers between devices: 69.2 us -> none  [local(): lax.psum_scatter(partial_value, ('col', 'layer'), scatter_dimension=1, ti...]
    mul x4 -> x0, local copies, waits for them, and re-layouts: 24.7 us -> none  [apply_pattern(): masked = shaped * pattern[:, None, :, None].astype(jnp.bfloat16)]
    dot_general x4 -> x0, matrix products: 18.1 us -> none  [local(): piece = jnp.dot(left, current, preferred_element_type=jnp.float32)]
    mul x2 -> x0, other arithmetic: 9.9 us -> none  [apply_pattern(): masked = shaped * pattern[:, None, :, None].astype(jnp.bfloat16)]
    broadcast_in_dim x1 -> x0, local copies, waits for them, and re-layouts: 4.8 us -> none  [local(): partial_value = jnp.zeros((left_rows, range_cols * cycle_size), jnp.float32)]
    ppermute x3 -> x0, starting transfers between devices: 3.03 us -> none  [from_behind(): return lax.ppermute(x, axis, [(i, (i + by) % size) for i in range(size)])]
  transfers between devices with their start and end apart: 4 -> 0, of which waited for: 4 -> 0; matrix products, arithmetic and copies ran while one was open for 17% -> 0% of each run, Pallas kernels for 0% -> 0%
where the time goes in v2:
time: 131 us
  Pallas kernels  108 us (82%)
  between operations  14.8 us (11%)
  local copies, waits for them, and re-layouts  5.05 us (4%)
  other arithmetic  2.16 us (2%)
    pallas_call x1, Pallas kernels, run(): pl.pallas_call(kernel, out_shape=(jax.ShapeDtypeStruct((rows, width // 2)...  108 us

profile of v2, /device:TPU:0, one launch (start us, length us, event | category | flops | bytes accessed | tf_op | source)
XLA Modules:
  0.0 130.6 jit_solution(16264783305397208548)
XLA Ops:
  6.5 0.0 copy-start.5
  6.5 0.0 copy-start.4
  6.5 0.0 copy-start
  6.5 0.9 copy.14
  7.5 0.1 reshape.349
  7.6 0.3 reduce-window.9
  7.9 0.1 slice.13
  8.0 0.1 slice_reduce_fusion
  8.2 0.1 reshape.354
  8.3 0.1 bitcast_subtract_fusion
  8.4 0.1 reshape.348
  8.6 0.1 broadcast.301
  8.6 0.1 reshape.352
  8.7 0.1 reshape.351
  8.8 0.1 broadcast_add_fusion
  8.9 1.4 %fusion.1 = pred[]{:T(512)} fusion(s32[4,1]{1,0:T(4,128)} %constant.99, s32[4,64]{1,0:T(4,128)S(1)} %broadcast_add_fusion), kind=kLoop, calls=%fused_computation.27 | loop fusion | flops 7 | bytes 33 | tf_op jit(solution)/shard_map/reduce_or | solution.py:374
  10.9 0.1 pad.6.clone
  11.0 0.1 add_add_fusion
  11.1 0.6 reshape.353.code_ref
  11.7 0.1 select_reduce_fusion
  11.9 0.6 reshape.355.pack_ref
  12.5 108.4 %sparse_product.1 = (bf16[1024,256]{1,0:T(8,128)(2,1)S(1)}, s32[8,128]{1,0:T(8,128)}) custom-call(bf16[1024,2048]{1,0:T(8,128)(2,1)} %left_ref.1, s32[16,32]{1,0:T(8,128)} %lpat_ref.1, bf16[2048,512]{1,0:T(8,128)(2,1)} %right_ref.1, s32[8,128]{1,0:T(8,128)} %reshape.353.code_ref, s32[6,128]{1,0:T(8,128)} %reshape.355.pack_ref), custom_call_target="tpu_custom_call" | custom-call | tf_op jit(solution)/shard_map/sparse_product/pallas_call | solution.py:334
  120.9 1.2 slice.16
  122.7 0.0 copy-done.5
  122.7 0.0 copy-done.4
  122.8 0.0 copy-done
  122.8 0.2 conditional.1
  123.0 0.8 copy.22
  (7 shorter events, 0.1 us)
Async XLA Ops:
  6.5 116.2 %copy-start.5 = (s32[32,8]{0,1:T(8,128)S(1)}, s32[32,8]{0,1:T(8,128)}, u32[]{:S(2)}) copy-start(s32[32,8]{0,1:T(8,128)} %param.10) | copy-start | bytes 3076
  6.5 116.2 %copy-start.4 = (s32[16,32]{1,0:T(8,128)S(1)}, s32[16,32]{1,0:T(8,128)}, u32[]{:S(2)}) copy-start(s32[16,32]{1,0:T(8,128)} %lpat_ref.1) | copy-start | bytes 6148
  6.5 116.2 %copy-start = (bf16[2048,512]{1,0:T(8,128)(2,1)S(1)}, bf16[2048,512]{1,0:T(8,128)(2,1)}, u32[]{:S(2)}) copy-start(bf16[2048,512]{1,0:T(8,128)(2,1)} %right_ref.1) | copy-start | bytes 6291460

commit v3 on v2

--- a/solution.py
+++ b/solution.py
@@ -17,6 +17,21 @@
 def from_behind(x, axis, by):
     size = lax.axis_size(axis)
     return lax.ppermute(x, axis, [(i, (i + by) % size) for i in range(size)])
+
+
+def scatter_sum(partial_value):
+    axes = ("col", "layer")
+    size = lax.axis_size(axes)
+    width = partial_value.shape[1] // size
+    here = lax.axis_index("col") * lax.axis_size("layer") + lax.axis_index("layer")
+
+    def share(owner):
+        return lax.dynamic_slice_in_dim(partial_value, (owner % size) * width, width, 1)
+
+    total = share(here)
+    for away in range(1, size):
+        total = total + from_behind(share(here + away), axes, away)
+    return total
 
 
 def apply_pattern(values, pattern):
@@ -42,8 +57,7 @@
         owner = (position - step) % cycle_size
         piece = jnp.dot(left, current, preferred_element_type=jnp.float32)
         partial_value = lax.dynamic_update_slice_in_dim(partial_value, piece, owner * range_cols, 1)
-    reduced = lax.psum_scatter(partial_value, ("col", "layer"), scatter_dimension=1, tiled=True)
-    return reduced.astype(jnp.bfloat16)
+    return scatter_sum(partial_value).astype(jnp.bfloat16)
 
 
 def turn(tile):
@@ -59,7 +73,7 @@
 
 
 def kernel(left_ref, lpat_ref, right_ref, code_ref, pack_ref, out_ref, flag_ref,
-           masked, tiled, held, current, wide, part, swapped, got, done, codes, scalars, flags,
+           masked, tiled, held, current, wide, part, swapped, got, done, codes, scalars, flags, flag_scalars,
            zsend, zrecv, xsend, xrecv, rsend, rrecv, fsend, frecv, csend, crecv, ssem, gsend, grecv):
     z = lax.axis_index("row")
     col = lax.axis_index("col")
@@ -285,7 +299,11 @@
 
     for i in range(1, 4):
         flag_from(i).wait_recv()
-    flag_ref[...] = jnp.maximum(jnp.maximum(flags[2], flags[3]), jnp.maximum(flags[4], flags[5]))
+    flags[6] = jnp.maximum(jnp.maximum(flags[2], flags[3]), jnp.maximum(flags[4], flags[5]))
+    to_flag = pltpu.make_async_copy(flags.at[6], flag_scalars, ssem)
+    to_flag.start()
+    to_flag.wait()
+    flag_ref[0] = flag_scalars[6, 0]
     pair.wait_send()
     for i in range(1, 4):
         spread_flag(i).wait_send()
@@ -334,9 +352,9 @@
     return pl.pallas_call(
         kernel,
         out_shape=(jax.ShapeDtypeStruct((rows, width // 2), jnp.bfloat16),
-                   jax.ShapeDtypeStruct((8, 128), jnp.int32)),
+                   jax.ShapeDtypeStruct((1,), jnp.int32)),
         in_specs=[vmem, vmem, vmem, vmem, smem],
-        out_specs=(vmem, vmem),
+        out_specs=(vmem, smem),
         scratch_shapes=[
             pltpu.VMEM(left.shape, jnp.bfloat16),
             pltpu.VMEM((tiles, BLOCK, 128), jnp.bfloat16),
@@ -349,7 +367,8 @@
             pltpu.VMEM((units, eighth, 128), jnp.bfloat16),
             pltpu.VMEM((4, 8, 128), jnp.int32),
             pltpu.SMEM((4, 8, 128), jnp.int32),
-            pltpu.VMEM((6, 8, 128), jnp.int32),
+            pltpu.VMEM((7, 8, 128), jnp.int32),
+            pltpu.SMEM((8, 128), jnp.int32),
             dma((2, 4, CHUNKS)), dma((4, CHUNKS)),
             dma((units, 4)), dma((units, 4)), dma((units, 3)), dma((units, 3)),
             dma((units,)), dma((2, 4, 2)), dma((3,)), dma((4,)), dma, dma((4,)), dma((4,)),
@@ -383,7 +402,7 @@
     keep = ((source - index) % 2 == 0).astype(jnp.int32)
     pack = jnp.stack([source // 2, keep, 1 - keep]).reshape(6, 128)
     out, flag = run(left, lpat, right, code, pack)
-    return lax.cond(flag[6, 0] > 0, local_general, lambda *_: out, left, lpat, right, rpat)
+    return lax.cond(flag[0] > 0, local_general, lambda *_: out, left, lpat, right, rpat)
 
 
 def solution(mesh):

time: 131 us -> 116 us (0.89)
  between operations: 14.8 us -> 1.36 us
where the time goes in v3:
time: 116 us
  Pallas kernels  108 us (93%)
  local copies, waits for them, and re-layouts  3.87 us (3%)
  other arithmetic  2.16 us (2%)
  between operations  1.36 us (1%)
    pallas_call x1, Pallas kernels, run(): pl.pallas_call(kernel, out_shape=(jax.ShapeDtypeStruct((rows, width // 2)...  108 us

profile of v3, /device:TPU:0, one launch (start us, length us, event | category | flops | bytes accessed | tf_op | source)
XLA Modules:
  0.0 116.0 jit_solution(16808339130347100302)
XLA Ops:
  0.0 0.0 copy-start.7
  0.0 0.0 copy-start.6
  0.0 0.0 copy-start.1
  0.0 0.9 copy.14
  0.9 0.1 reshape.349
  1.1 0.3 reduce-window.9
  1.4 0.1 slice.10
  1.5 0.1 slice_reduce_fusion
  1.6 0.1 reshape.354
  1.8 0.1 bitcast_subtract_fusion
  1.8 0.1 reshape.348
  2.0 0.1 broadcast.309
  2.1 0.1 reshape.352
  2.2 0.1 reshape.351
  2.3 0.1 broadcast_add_fusion
  2.4 1.4 %fusion.1 = pred[]{:T(512)} fusion(s32[4,1]{1,0:T(4,128)} %constant.153, s32[4,64]{1,0:T(4,128)S(1)} %broadcast_add_fusion), kind=kLoop, calls=%fused_computation.35 | loop fusion | flops 7 | bytes 33 | tf_op jit(solution)/shard_map/reduce_or | solution.py:393
  4.4 0.1 pad.6.clone
  4.5 0.1 add_add_fusion
  4.5 0.6 reshape.353.code_ref
  5.2 0.1 select_reduce_fusion
  5.3 0.6 reshape.355.pack_ref
  5.9 108.4 %sparse_product.1 = (bf16[1024,256]{1,0:T(8,128)(2,1)S(1)}, s32[1]{0:T(128)}) custom-call(bf16[1024,2048]{1,0:T(8,128)(2,1)} %left_ref.1, s32[16,32]{1,0:T(8,128)} %lpat_ref.1, bf16[2048,512]{1,0:T(8,128)(2,1)} %right_ref.1, s32[8,128]{1,0:T(8,128)} %reshape.353.code_ref, s32[6,128]{1,0:T(8,128)} %reshape.355.pack_ref), custom_call_target="tpu_custom_call" | custom-call | tf_op jit(solution)/shard_map/sparse_product/pallas_call | solution.py:352
  114.9 0.0 copy-done.7
  114.9 0.0 copy-done.6
  114.9 0.0 copy-done.1
  115.0 0.2 conditional.1
  115.2 0.8 copy.22
  (7 shorter events, 0.1 us)
Async XLA Ops:
  0.0 114.9 %copy-start.7 = (s32[32,8]{0,1:T(8,128)S(1)}, s32[32,8]{0,1:T(8,128)}, u32[]{:S(2)}) copy-start(s32[32,8]{0,1:T(8,128)} %param.10) | copy-start | bytes 3076
  0.0 114.9 %copy-start.6 = (s32[16,32]{1,0:T(8,128)S(1)}, s32[16,32]{1,0:T(8,128)}, u32[]{:S(2)}) copy-start(s32[16,32]{1,0:T(8,128)} %lpat_ref.1) | copy-start | bytes 6148
  0.0 114.9 %copy-start.1 = (bf16[2048,512]{1,0:T(8,128)(2,1)S(1)}, bf16[2048,512]{1,0:T(8,128)(2,1)}, u32[]{:S(2)}) copy-start(bf16[2048,512]{1,0:T(8,128)(2,1)} %right_ref.1) | copy-start | bytes 6291460

commit v4 on v3

--- a/solution.py
+++ b/solution.py
@@ -9,8 +9,10 @@
 
 MESH = pl.DeviceIdType.MESH
 BLOCK = 64
-CAP = 160
-CHUNKS = 8
+CAP = 148
+SPARE = 16
+EDGES = (0, 10, 20, 30, 40, 50, 58, 66, 74)
+CHUNKS = len(EDGES) - 1
 READY = (3, 5, 7, 8)
 
 
@@ -72,15 +74,68 @@
     return first + second
 
 
+def prepare(pattern_ref, code_ref, pack_ref):
+    kblocks, cols = pattern_ref.shape
+    count = kblocks * cols
+    per_strip = 2 * kblocks
+
+    def iota(shape, axis):
+        return lax.broadcasted_iota(jnp.int32, shape, axis)
+
+    block = iota((cols, count), 1)
+    choose = iota((cols, count), 0) == 2 * (block // per_strip) + block % 2
+    spread = jnp.dot(pattern_ref[...].astype(jnp.float32), jnp.where(choose, 1.0, 0.0),
+                     preferred_element_type=jnp.float32)
+    mine = iota((kblocks, count), 0) == (iota((kblocks, count), 1) % per_strip) // 2
+    present = jnp.sum(jnp.where(mine, spread, 0.0), axis=0, keepdims=True)
+    before = jnp.where(iota((count, count), 0) < iota((count, count), 1), 1.0, 0.0)
+    slot = jnp.dot(jnp.broadcast_to(present, (8, count)), before,
+                   preferred_element_type=jnp.float32)[0:1].astype(jnp.int32)
+    index = iota((1, count), 1)
+    there = present > 0.5
+    place = jnp.where(slot < CAP, slot, jnp.maximum(2 * CAP + SPARE - 1 - slot, CAP))
+    same = place % 2 == index % 2
+
+    eye = iota((count, count), 0) == iota((count, count), 1)
+    column = jnp.sum(jnp.where(eye, jnp.where(there, place, -1).astype(jnp.float32), 0.0), axis=1, keepdims=True)
+    hit = jnp.where(column.astype(jnp.int32) == iota((count, count), 1), 1.0, 0.0)
+    source = jnp.sum(hit * iota((count, count), 0).astype(jnp.float32), axis=0, keepdims=True).astype(jnp.int32)
+    used = jnp.sum(hit, axis=0, keepdims=True) > 0.5
+    source = jnp.clip(source, 0, count - 1)
+    level = source % 2 == index % 2
+
+    total = jnp.sum(present, axis=1, keepdims=True)
+    over = jnp.where(total > CAP + SPARE, 1.0, 0.0)
+    for g in range(cols // 2 - 1):
+        upto = jnp.sum(jnp.where(index < per_strip * (g + 1), present, 0.0), axis=1, keepdims=True)
+        over = jnp.maximum(over, jnp.where(upto > 2 * EDGES[READY[g]], 1.0, 0.0))
+    weight = jnp.broadcast_to(total + 4096.0 * over, (1, count)).astype(jnp.int32)
+
+    def put(ref, row, value):
+        ref[row:row + 1, :] = value[:, :128]
+        ref[row + 1:row + 2, :] = value[:, 128:]
+
+    put(code_ref, 0, jnp.where(there, place // 2, 0))
+    put(code_ref, 2, jnp.where(there & same, 1, 0))
+    put(code_ref, 4, jnp.where(there & jnp.logical_not(same), 1, 0))
+    put(code_ref, 6, weight)
+    put(pack_ref, 0, source // 2)
+    put(pack_ref, 2, jnp.where(used & level, 1, 0))
+    put(pack_ref, 4, jnp.where(used & jnp.logical_not(level), 1, 0))
+    put(pack_ref, 6, jnp.zeros((1, count), jnp.int32))
+
+
 def kernel(left_ref, lpat_ref, right_ref, code_ref, pack_ref, out_ref, flag_ref,
-           masked, tiled, held, current, wide, part, swapped, got, done, codes, scalars, flags, flag_scalars,
-           zsend, zrecv, xsend, xrecv, rsend, rrecv, fsend, frecv, csend, crecv, ssem, gsend, grecv):
+           masked, tiled, held, spill, foreign, lent, current, wide, part, swapped, got, done,
+           codes, other_codes, scalars, flags, flag_scalars,
+           zsend, zrecv, xsend, xrecv, rsend, rrecv, fsend, frecv, csend, crecv, ssem, gsend, grecv,
+           spill_send, spill_recv, lend_send, lend_recv):
     z = lax.axis_index("row")
     col = lax.axis_index("col")
     layer = lax.axis_index("layer")
     core = lax.rem(layer, 2)
     chip = col * 2 + lax.div(layer, 2)
-    tiles = CAP // 2 // CHUNKS
+    tiles, last = CAP // 2, CAP // 2 - SPARE // 2
     rows = left_ref.shape[0]
     quarter, eighth = rows // 4, rows // 8
     kblocks = right_ref.shape[0] // BLOCK
@@ -115,22 +170,39 @@
 
     lax.fori_loop(0, kblocks, cut, 0)
 
+    def packed(t):
+        row, e = lax.div(t, 64), lax.rem(t, 64) * 2
+        return join(
+            tiled[pack_ref[row, e]], tiled[pack_ref[row, e + 1]],
+            pack_ref[2 + row, e].astype(jnp.float32), pack_ref[4 + row, e].astype(jnp.float32),
+            pack_ref[2 + row, e + 1].astype(jnp.float32), pack_ref[4 + row, e + 1].astype(jnp.float32))
+
     def pack(c):
         def one(t, carry):
-            row, e = lax.div(t, 64), lax.rem(t, 64) * 2
-            held[z, t] = join(
-                tiled[pack_ref[row, e]], tiled[pack_ref[row, e + 1]],
-                pack_ref[2 + row, e].astype(jnp.float32), pack_ref[4 + row, e].astype(jnp.float32),
-                pack_ref[2 + row, e + 1].astype(jnp.float32), pack_ref[4 + row, e + 1].astype(jnp.float32))
+            held[z, t] = packed(t)
             return carry
-        lax.fori_loop(c * tiles, (c + 1) * tiles, one, 0)
+
+        def with_foreign(t, carry):
+            held[z, t] = packed(t) + foreign[t - last]
+            return carry
+        lax.fori_loop(EDGES[c], EDGES[c + 1], one if c < CHUNKS - 1 else with_foreign, 0)
+
+    def pack_spill(t, carry):
+        spill[t] = packed(tiles + t)
+        return carry
+
+    def span(c):
+        return pl.ds(EDGES[c], EDGES[c + 1] - EDGES[c])
+
+    def lend(r):
+        return remote(held.at[order(r), pl.ds(last, SPARE // 2)], lent.at[r], lend_send.at[r], lend_recv.at[r], partner)
 
     def up(j, c):
-        piece = held.at[j, pl.ds(c * tiles, tiles)]
+        piece = held.at[j, span(c)]
         return remote(piece, piece, zsend.at[0, j, c], zrecv.at[j, c], above)
 
     def down(j, c):
-        piece = held.at[j, pl.ds(c * tiles, tiles)]
+        piece = held.at[j, span(c)]
         return remote(piece, piece, zsend.at[1, j, c], zrecv.at[j, c], below)
 
     def tell(i):
@@ -144,7 +216,10 @@
     pl.semaphore_wait(barrier, 7)
     for i in range(1, 4):
         tell(i).start()
+    spilled = remote(spill, foreign, spill_send, spill_recv, partner)
     for c in range(CHUNKS):
+        if c == CHUNKS - 1:
+            spilled.wait_recv()
         if c > 0:
             pack(c)
 
@@ -155,6 +230,10 @@
         @pl.when(has_below)
         def _():
             down(z, c).start()
+
+        if c == 0:
+            lax.fori_loop(0, SPARE // 2, pack_spill, 0)
+            spilled.start()
 
     depth = left_ref.shape[1]
     spread = (lax.broadcasted_iota(jnp.int32, (depth // BLOCK, depth), 1) // BLOCK
@@ -170,8 +249,7 @@
     to_scalars = pltpu.make_async_copy(codes, scalars, ssem)
     to_scalars.start()
     to_scalars.wait()
-    flags[0] = jnp.maximum(jnp.maximum(codes[0], codes[1]), jnp.maximum(codes[2], codes[3]))
-    pair = remote(flags.at[0], flags.at[1], gsend.at[0], grecv.at[0], partner)
+    pair = remote(codes, other_codes, gsend.at[0], grecv.at[0], partner)
     pair.start()
 
     def spread_flag(i):
@@ -211,7 +289,13 @@
             current[t] = held[j, t]
             return carry
         first = 0 if g == 0 else READY[g - 1]
-        lax.fori_loop(first * tiles, READY[g] * tiles, fetch, 0)
+        if g == strips - 1:
+            lend(r).start()
+        lax.fori_loop(EDGES[first], EDGES[READY[g]], fetch, 0)
+        if g == strips - 1:
+            lend(r).wait_recv()
+            for t in range(SPARE // 2):
+                current[tiles + t] = lent[r, t]
 
         def one(k, carry):
             row, e = g // 2, (g % 2) * 64 + 2 * k
@@ -291,7 +375,8 @@
         return carry
 
     pair.wait_recv()
-    flags[2] = jnp.maximum(flags[0], flags[1])
+    sums = [codes[j] + other_codes[j] for j in range(4)]
+    flags[2] = jnp.maximum(jnp.maximum(sums[0], sums[1]), jnp.maximum(sums[2], sums[3]))
     for i in range(1, 4):
         spread_flag(i).start()
     lax.fori_loop(0, 4, rank, 0)
@@ -305,6 +390,7 @@
     to_flag.wait()
     flag_ref[0] = flag_scalars[6, 0]
     pair.wait_send()
+    spilled.wait_send()
     for i in range(1, 4):
         spread_flag(i).wait_send()
         tell(i).wait_send()
@@ -319,6 +405,9 @@
     def drain(r, carry):
         for g in range(strips):
             n = r * strips + g
+
+            if g == 0:
+                lend(r).wait_send()
 
             @pl.when((order(r) != chip) | (core != g // 2))
             def _():
@@ -359,12 +448,16 @@
             pltpu.VMEM(left.shape, jnp.bfloat16),
             pltpu.VMEM((tiles, BLOCK, 128), jnp.bfloat16),
             pltpu.VMEM((4, CAP // 2, BLOCK, 128), jnp.bfloat16),
-            pltpu.VMEM((CAP // 2, BLOCK, 128), jnp.bfloat16),
+            pltpu.VMEM((SPARE // 2, BLOCK, 128), jnp.bfloat16),
+            pltpu.VMEM((SPARE // 2, BLOCK, 128), jnp.bfloat16),
+            pltpu.VMEM((4, SPARE // 2, BLOCK, 128), jnp.bfloat16),
+            pltpu.VMEM((CAP // 2 + SPARE // 2, BLOCK, 128), jnp.bfloat16),
             pltpu.VMEM((right.shape[0], 128), jnp.bfloat16),
             pltpu.VMEM((units, 4, 2, eighth, 128), jnp.float32),
             pltpu.VMEM((units, 4, eighth, 128), jnp.float32),
             pltpu.VMEM((units, 3, eighth, 128), jnp.float32),
             pltpu.VMEM((units, eighth, 128), jnp.bfloat16),
+            pltpu.VMEM((4, 8, 128), jnp.int32),
             pltpu.VMEM((4, 8, 128), jnp.int32),
             pltpu.SMEM((4, 8, 128), jnp.int32),
             pltpu.VMEM((7, 8, 128), jnp.int32),
@@ -372,6 +465,7 @@
             dma((2, 4, CHUNKS)), dma((4, CHUNKS)),
             dma((units, 4)), dma((units, 4)), dma((units, 3)), dma((units, 3)),
             dma((units,)), dma((2, 4, 2)), dma((3,)), dma((4,)), dma, dma((4,)), dma((4,)),
+            dma, dma, dma((4,)), dma((4,)),
         ],
         compiler_params=pltpu.CompilerParams(
             collective_id=0, has_side_effects=True, vmem_limit_bytes=56 * 2**20),
@@ -380,29 +474,12 @@
 
 
 def local_packed(left, lpat, right, rpat):
-    kblocks, cols = rpat.shape
-    present = rpat.reshape(kblocks, cols // 2, 2).transpose(1, 0, 2).reshape(-1)
-    count = present.size
-    upto = jnp.cumsum(present)
-    slot = upto - present
-    index = jnp.arange(count, dtype=jnp.int32)
-    there = present > 0
-    same = (slot - index) % 2 == 0
-    ends = upto.reshape(cols // 2, -1)[:, -1]
-    room = jnp.array([ready * (CAP // CHUNKS) for ready in READY], jnp.int32)
-    over = jnp.any(ends > room).astype(jnp.int32)
-    code = jnp.stack([
-        jnp.where(there, jnp.minimum(slot // 2, CAP // 2 - 1), 0),
-        (there & same).astype(jnp.int32),
-        (there & jnp.logical_not(same)).astype(jnp.int32),
-        jnp.broadcast_to(over, (count,)),
-    ]).reshape(8, 128)
-    hit = (slot[None, :] == index[:, None]) & there[None, :]
-    source = jnp.sum(jnp.where(hit, index[None, :], 0), axis=1)
-    keep = ((source - index) % 2 == 0).astype(jnp.int32)
-    pack = jnp.stack([source // 2, keep, 1 - keep]).reshape(6, 128)
+    table = jax.ShapeDtypeStruct((8, 128), jnp.int32)
+    vmem = pl.BlockSpec(memory_space=pltpu.VMEM)
+    code, pack = pl.pallas_call(
+        prepare, out_shape=(table, table), in_specs=[vmem], out_specs=(vmem, vmem), name="places")(rpat)
     out, flag = run(left, lpat, right, code, pack)
-    return lax.cond(flag[0] > 0, local_general, lambda *_: out, left, lpat, right, rpat)
+    return lax.cond(flag[0] > 2 * CAP, local_general, lambda *_: out, left, lpat, right, rpat)
 
 
 def solution(mesh):

time: 116 us -> 109 us (0.940)
  other arithmetic: 2.16 us -> 0 us
  Pallas kernels: 108 us -> 106 us
  local copies, waits for them, and re-layouts: 3.87 us -> 2.32 us
    pallas_call x1, Pallas kernels: 108 us -> 104 us  [run(): pl.pallas_call(kernel, out_shape=(jax.ShapeDtypeStruct((rows, width // 2)...]
    reshape x6 -> x0, local copies, waits for them, and re-layouts: 2.56 us -> none  [the longest x3 1.22 us: local_packed(): present = rpat.reshape(kblocks, cols // 2, 2).transpose(1, 0, 2).reshape(-1)]
    pallas_call x0 -> x1, Pallas kernels: none -> 1.71 us  [local_packed(): pl.pallas_call(prepare, out_shape=(table, table), in_specs=[vmem], out_sp...]
    unnamed x7 -> x8, local copies, waits for them, and re-layouts: 0.81 us -> 2.32 us
    reduce_or x1 -> x0, other arithmetic: 1.39 us -> none  [local_packed(): over = jnp.any(ends > room).astype(jnp.int32)]
where the time goes in v4:
time: 109 us
  Pallas kernels  106 us (97%)
  local copies, waits for them, and re-layouts  2.32 us (2%)
    pallas_call x1, Pallas kernels, run(): pl.pallas_call(kernel, out_shape=(jax.ShapeDtypeStruct((rows, width // 2)...  104 us
    unnamed x8, local copies, waits for them, and re-layouts  2.32 us

profile of v4, /device:TPU:0, one launch (start us, length us, event | category | flops | bytes accessed | tf_op | source)
XLA Modules:
  0.0 109.0 jit_solution(1286132810354527778)
XLA Ops:
  0.0 0.0 copy-start.7
  0.0 0.0 copy-start.6
  0.0 0.0 copy-start.1
  0.0 1.5 %copy.8.pattern_ref = s32[32,8]{1,0:T(8,128)} copy(s32[32,8]{0,1:T(8,128)} %param.9) | data formatting | bytes 2048 | tf_op args[3]
  1.5 1.7 %places.1 = (s32[8,128]{1,0:T(8,128)}, s32[8,128]{1,0:T(8,128)}) custom-call(s32[32,8]{1,0:T(8,128)} %copy.8.pattern_ref), custom_call_target="tpu_custom_call" | custom-call | tf_op jit(solution)/shard_map/places/pallas_call | solution.py:479
  3.2 104.0 %sparse_product.1 = (bf16[1024,256]{1,0:T(8,128)(2,1)S(1)}, s32[1]{0:T(128)}) custom-call(bf16[1024,2048]{1,0:T(8,128)(2,1)} %left_ref.1, s32[16,32]{1,0:T(8,128)} %lpat_ref.1, bf16[2048,512]{1,0:T(8,128)(2,1)} %right_ref.1, s32[8,128]{1,0:T(8,128)} %get-tuple-element.25.code_ref, s32[8,128]{1,0:T(8,128)} %get-tuple-element.26.pack_ref), custom_call_target="tpu_custom_call" | custom-call | tf_op jit(solution)/shard_map/sparse_product/pallas_call | solution.py:441
  107.9 0.0 copy-done.7
  107.9 0.0 copy-done.6
  107.9 0.0 copy-done.1
  107.9 0.2 conditional.1
  108.2 0.8 copy.16
Async XLA Ops:
  0.0 107.9 %copy-start.7 = (s32[32,8]{0,1:T(8,128)S(1)}, s32[32,8]{0,1:T(8,128)}, u32[]{:S(2)}) copy-start(s32[32,8]{0,1:T(8,128)} %param.9) | copy-start | bytes 3076
  0.0 107.9 %copy-start.6 = (s32[16,32]{1,0:T(8,128)S(1)}, s32[16,32]{1,0:T(8,128)}, u32[]{:S(2)}) copy-start(s32[16,32]{1,0:T(8,128)} %lpat_ref.1) | copy-start | bytes 6148
  0.0 107.9 %copy-start.1 = (bf16[2048,512]{1,0:T(8,128)(2,1)S(1)}, bf16[2048,512]{1,0:T(8,128)(2,1)}, u32[]{:S(2)}) copy-start(bf16[2048,512]{1,0:T(8,128)(2,1)} %right_ref.1) | copy-start | bytes 6291460

commit v5 on v4

--- a/solution.py
+++ b/solution.py
@@ -66,12 +66,9 @@
     return jnp.concatenate([tile[:, BLOCK:], tile[:, :BLOCK]], axis=1)
 
 
-def join(a, b, stay_a, turn_a, stay_b, turn_b):
+def join(a, b):
     left = jnp.where(lax.broadcasted_iota(jnp.int32, (1, 128), 1) < BLOCK, 1.0, 0.0)
-    right = 1.0 - left
-    first = a * (left * stay_a).astype(jnp.bfloat16) + turn(a) * (left * turn_a).astype(jnp.bfloat16)
-    second = b * (right * stay_b).astype(jnp.bfloat16) + turn(b) * (right * turn_b).astype(jnp.bfloat16)
-    return first + second
+    return a * left.astype(jnp.bfloat16) + b * (1.0 - left).astype(jnp.bfloat16)
 
 
 def prepare(pattern_ref, code_ref, pack_ref):
@@ -115,14 +112,12 @@
         ref[row:row + 1, :] = value[:, :128]
         ref[row + 1:row + 2, :] = value[:, 128:]
 
-    put(code_ref, 0, jnp.where(there, place // 2, 0))
-    put(code_ref, 2, jnp.where(there & same, 1, 0))
-    put(code_ref, 4, jnp.where(there & jnp.logical_not(same), 1, 0))
-    put(code_ref, 6, weight)
-    put(pack_ref, 0, source // 2)
-    put(pack_ref, 2, jnp.where(used & level, 1, 0))
-    put(pack_ref, 4, jnp.where(used & jnp.logical_not(level), 1, 0))
-    put(pack_ref, 6, jnp.zeros((1, count), jnp.int32))
+    tiles = (CAP + SPARE) // 2
+    put(code_ref, 0, jnp.where(there, place // 2 + jnp.where(same, 0, tiles), 2 * tiles))
+    put(code_ref, 2, weight)
+    put(pack_ref, 0, jnp.where(used, source // 2 + jnp.where(level, 0, count // 2), count))
+    for ref, row in ((code_ref, 4), (code_ref, 6), (pack_ref, 2), (pack_ref, 4), (pack_ref, 6)):
+        put(ref, row, jnp.zeros((1, count), jnp.int32))
 
 
 def kernel(left_ref, lpat_ref, right_ref, code_ref, pack_ref, out_ref, flag_ref,
@@ -135,7 +130,7 @@
     layer = lax.axis_index("layer")
     core = lax.rem(layer, 2)
     chip = col * 2 + lax.div(layer, 2)
-    tiles, last = CAP // 2, CAP // 2 - SPARE // 2
+    tiles, last, most = CAP // 2, CAP // 2 - SPARE // 2, CAP // 2 + SPARE // 2
     rows = left_ref.shape[0]
     quarter, eighth = rows // 4, rows // 8
     kblocks = right_ref.shape[0] // BLOCK
@@ -165,17 +160,18 @@
 
     def cut(k, carry):
         for m in range(strips):
-            tiled[m * kblocks + k] = right_ref[pl.ds(pl.multiple_of(k * BLOCK, BLOCK), BLOCK), m * 128:(m + 1) * 128]
+            tile = right_ref[pl.ds(pl.multiple_of(k * BLOCK, BLOCK), BLOCK), m * 128:(m + 1) * 128]
+            tiled[m * kblocks + k] = tile
+            tiled[(strips + m) * kblocks + k] = turn(tile)
         return carry
 
-    lax.fori_loop(0, kblocks, cut, 0)
+    lax.fori_loop(0, kblocks, cut, 0, unroll=2)
+    tiled[2 * strips * kblocks] = jnp.zeros((BLOCK, 128), jnp.bfloat16)
+    current[2 * most] = jnp.zeros((BLOCK, 128), jnp.bfloat16)
 
     def packed(t):
         row, e = lax.div(t, 64), lax.rem(t, 64) * 2
-        return join(
-            tiled[pack_ref[row, e]], tiled[pack_ref[row, e + 1]],
-            pack_ref[2 + row, e].astype(jnp.float32), pack_ref[4 + row, e].astype(jnp.float32),
-            pack_ref[2 + row, e + 1].astype(jnp.float32), pack_ref[4 + row, e + 1].astype(jnp.float32))
+        return join(tiled[pack_ref[row, e]], tiled[pack_ref[row, e + 1]])
 
     def pack(c):
         def one(t, carry):
@@ -287,22 +283,22 @@
 
         def fetch(t, carry):
             current[t] = held[j, t]
+            current[most + t] = turn(held[j, t])
             return carry
         first = 0 if g == 0 else READY[g - 1]
         if g == strips - 1:
             lend(r).start()
-        lax.fori_loop(EDGES[first], EDGES[READY[g]], fetch, 0)
+        lax.fori_loop(EDGES[first], EDGES[READY[g]], fetch, 0, unroll=2)
         if g == strips - 1:
             lend(r).wait_recv()
             for t in range(SPARE // 2):
                 current[tiles + t] = lent[r, t]
+                current[most + tiles + t] = turn(lent[r, t])
 
         def one(k, carry):
             row, e = g // 2, (g % 2) * 64 + 2 * k
             wide[pl.ds(pl.multiple_of(k * BLOCK, BLOCK), BLOCK), :] = join(
-                current[scalars[j, row, e]], current[scalars[j, row, e + 1]],
-                scalars[j, 2 + row, e].astype(jnp.float32), scalars[j, 4 + row, e].astype(jnp.float32),
-                scalars[j, 2 + row, e + 1].astype(jnp.float32), scalars[j, 4 + row, e + 1].astype(jnp.float32))
+                current[scalars[j, row, e]], current[scalars[j, row, e + 1]])
             return carry
         lax.fori_loop(0, kblocks, one, 0, unroll=4)
 
@@ -311,14 +307,16 @@
 
     def multiply(n):
         def one(i, carry):
-            q = lax.rem(chip + 1 + i, 4)
-            piece = jnp.dot(masked[pl.ds(pl.multiple_of(q * quarter, quarter), quarter), :], wide[...],
+            pair = lax.rem(lax.div(chip, 2) + 1 + i, 2)
+            piece = jnp.dot(masked[pl.ds(pl.multiple_of(pair * 2 * quarter, quarter), 2 * quarter), :], wide[...],
                             preferred_element_type=jnp.float32)
-            part[n, q, 0] = piece[:eighth]
-            part[n, q, 1] = piece[eighth:]
-            swap(n, q).start()
+            for k in range(2):
+                q = pair * 2 + k
+                part[n, q, 0] = piece[2 * k * eighth:(2 * k + 1) * eighth]
+                part[n, q, 1] = piece[(2 * k + 1) * eighth:(2 * k + 2) * eighth]
+                swap(n, q).start()
             return carry
-        lax.fori_loop(0, 4, one, 0)
+        lax.fori_loop(0, 2, one, 0)
 
     def scatter(n, i):
         return remote(part.at[n, other(i), core], got.at[n, 3 - i], rsend.at[n, i - 1], rrecv.at[n, 3 - i],
@@ -388,7 +386,7 @@
     to_flag = pltpu.make_async_copy(flags.at[6], flag_scalars, ssem)
     to_flag.start()
     to_flag.wait()
-    flag_ref[0] = flag_scalars[6, 0]
+    flag_ref[0] = flag_scalars[2, 0]
     pair.wait_send()
     spilled.wait_send()
     for i in range(1, 4):
@@ -446,12 +444,12 @@
         out_specs=(vmem, smem),
         scratch_shapes=[
             pltpu.VMEM(left.shape, jnp.bfloat16),
-            pltpu.VMEM((tiles, BLOCK, 128), jnp.bfloat16),
+            pltpu.VMEM((2 * tiles + 1, BLOCK, 128), jnp.bfloat16),
             pltpu.VMEM((4, CAP // 2, BLOCK, 128), jnp.bfloat16),
             pltpu.VMEM((SPARE // 2, BLOCK, 128), jnp.bfloat16),
             pltpu.VMEM((SPARE // 2, BLOCK, 128), jnp.bfloat16),
             pltpu.VMEM((4, SPARE // 2, BLOCK, 128), jnp.bfloat16),
-            pltpu.VMEM((CAP // 2 + SPARE // 2, BLOCK, 128), jnp.bfloat16),
+            pltpu.VMEM((CAP + SPARE + 1, BLOCK, 128), jnp.bfloat16),
             pltpu.VMEM((right.shape[0], 128), jnp.bfloat16),
             pltpu.VMEM((units, 4, 2, eighth, 128), jnp.float32),
             pltpu.VMEM((units, 4, eighth, 128), jnp.float32),

time: 109 us -> 109 us (level)
  no operation moved by 1% of the time
where the time goes in v5:
time: 109 us; the launch traced here: 108 us
  Pallas kernels  105 us (96%)
  local copies, waits for them, and re-layouts  2.32 us (2%)
    pallas_call x1, Pallas kernels, run(): pl.pallas_call(kernel, out_shape=(jax.ShapeDtypeStruct((rows, width // 2)...  103 us
    unnamed x8, local copies, waits for them, and re-layouts  2.32 us

profile of v5, /device:TPU:0, one launch (start us, length us, event | category | flops | bytes accessed | tf_op | source)
XLA Modules:
  0.0 108.1 jit_solution(17618420298889496974)
XLA Ops:
  0.0 0.0 copy-start.7
  0.0 0.0 copy-start.6
  0.0 0.0 copy-start.1
  0.0 1.5 %copy.8.pattern_ref = s32[32,8]{1,0:T(8,128)} copy(s32[32,8]{0,1:T(8,128)} %param.9) | data formatting | bytes 2048 | tf_op args[3]
  1.5 1.7 %places.1 = (s32[8,128]{1,0:T(8,128)}, s32[8,128]{1,0:T(8,128)}) custom-call(s32[32,8]{1,0:T(8,128)} %copy.8.pattern_ref), custom_call_target="tpu_custom_call" | custom-call | tf_op jit(solution)/shard_map/places/pallas_call | solution.py:477
  3.2 103.2 %sparse_product.1 = (bf16[1024,256]{1,0:T(8,128)(2,1)S(1)}, s32[1]{0:T(128)}) custom-call(bf16[1024,2048]{1,0:T(8,128)(2,1)} %left_ref.1, s32[16,32]{1,0:T(8,128)} %lpat_ref.1, bf16[2048,512]{1,0:T(8,128)(2,1)} %right_ref.1, s32[8,128]{1,0:T(8,128)} %get-tuple-element.25.code_ref, s32[8,128]{1,0:T(8,128)} %get-tuple-element.26.pack_ref), custom_call_target="tpu_custom_call" | custom-call | tf_op jit(solution)/shard_map/sparse_product/pallas_call | solution.py:439
  107.0 0.0 copy-done.7
  107.0 0.0 copy-done.6
  107.1 0.0 copy-done.1
  107.1 0.2 conditional.1
  107.3 0.8 copy.16
Async XLA Ops:
  0.0 107.0 %copy-start.7 = (s32[32,8]{0,1:T(8,128)S(1)}, s32[32,8]{0,1:T(8,128)}, u32[]{:S(2)}) copy-start(s32[32,8]{0,1:T(8,128)} %param.9) | copy-start | bytes 3076
  0.0 107.0 %copy-start.6 = (s32[16,32]{1,0:T(8,128)S(1)}, s32[16,32]{1,0:T(8,128)}, u32[]{:S(2)}) copy-start(s32[16,32]{1,0:T(8,128)} %lpat_ref.1) | copy-start | bytes 6148
  0.0 107.1 %copy-start.1 = (bf16[2048,512]{1,0:T(8,128)(2,1)S(1)}, bf16[2048,512]{1,0:T(8,128)(2,1)}, u32[]{:S(2)}) copy-start(bf16[2048,512]{1,0:T(8,128)(2,1)} %right_ref.1) | copy-start | bytes 6291460

commit v6 on v5

--- a/solution.py
+++ b/solution.py
@@ -14,6 +14,7 @@
 EDGES = (0, 10, 20, 30, 40, 50, 58, 66, 74)
 CHUNKS = len(EDGES) - 1
 READY = (3, 5, 7, 8)
+LAG = 2
 
 
 def from_behind(x, axis, by):
@@ -72,7 +73,7 @@
 
 
 def prepare(pattern_ref, code_ref, pack_ref):
-    kblocks, cols = pattern_ref.shape
+    cols, kblocks = pattern_ref.shape
     count = kblocks * cols
     per_strip = 2 * kblocks
 
@@ -81,10 +82,10 @@
 
     block = iota((cols, count), 1)
     choose = iota((cols, count), 0) == 2 * (block // per_strip) + block % 2
-    spread = jnp.dot(pattern_ref[...].astype(jnp.float32), jnp.where(choose, 1.0, 0.0),
+    mine = iota((kblocks, count), 0) == (iota((kblocks, count), 1) % per_strip) // 2
+    spread = jnp.dot(pattern_ref[...].astype(jnp.float32), jnp.where(mine, 1.0, 0.0),
                      preferred_element_type=jnp.float32)
-    mine = iota((kblocks, count), 0) == (iota((kblocks, count), 1) % per_strip) // 2
-    present = jnp.sum(jnp.where(mine, spread, 0.0), axis=0, keepdims=True)
+    present = jnp.sum(jnp.where(choose, spread, 0.0), axis=0, keepdims=True)
     before = jnp.where(iota((count, count), 0) < iota((count, count), 1), 1.0, 0.0)
     slot = jnp.dot(jnp.broadcast_to(present, (8, count)), before,
                    preferred_element_type=jnp.float32)[0:1].astype(jnp.int32)
@@ -364,12 +365,12 @@
             expand(r, g)
             multiply(n)
             add_cores(n)
-            if g > 0:
-                finish(n - 1, r, g - 1)
+            if g >= LAG:
+                finish(n - LAG, r, g - LAG)
             else:
                 @pl.when(r > 0)
                 def _():
-                    finish(n - 1, r - 1, strips - 1)
+                    finish(n - LAG, r - 1, strips + g - LAG)
         return carry
 
     pair.wait_recv()
@@ -378,7 +379,8 @@
     for i in range(1, 4):
         spread_flag(i).start()
     lax.fori_loop(0, 4, rank, 0)
-    finish(4 * strips - 1, 3, strips - 1)
+    for g in range(strips - LAG, strips):
+        finish(3 * strips + g, 3, g)
 
     for i in range(1, 4):
         flag_from(i).wait_recv()
@@ -475,7 +477,7 @@
     table = jax.ShapeDtypeStruct((8, 128), jnp.int32)
     vmem = pl.BlockSpec(memory_space=pltpu.VMEM)
     code, pack = pl.pallas_call(
-        prepare, out_shape=(table, table), in_specs=[vmem], out_specs=(vmem, vmem), name="places")(rpat)
+        prepare, out_shape=(table, table), in_specs=[vmem], out_specs=(vmem, vmem), name="places")(rpat.T)
     out, flag = run(left, lpat, right, code, pack)
     return lax.cond(flag[0] > 2 * CAP, local_general, lambda *_: out, left, lpat, right, rpat)
 

time: 109 us -> 107 us (0.982)
  local copies, waits for them, and re-layouts: 2.32 us -> 0.81 us
    unnamed x8 -> x7, local copies, waits for them, and re-layouts: 2.32 us -> 0.81 us
where the time goes in v6:
time: 107 us
  Pallas kernels  105 us (98%)
    pallas_call x1, Pallas kernels, run(): pl.pallas_call(kernel, out_shape=(jax.ShapeDtypeStruct((rows, width // 2)...  103 us

profile of v6, /device:TPU:0, one launch (start us, length us, event | category | flops | bytes accessed | tf_op | source)
XLA Modules:
  0.0 106.7 jit_solution(17119198643672779960)
XLA Ops:
  0.0 0.0 copy-start.7
  0.0 0.0 copy-start.6
  0.0 0.0 copy-start.1
  0.0 1.8 %places.1 = (s32[8,128]{1,0:T(8,128)}, s32[8,128]{1,0:T(8,128)}) custom-call(s32[8,32]{1,0:T(8,128)} %bitcast.14), custom_call_target="tpu_custom_call" | custom-call | tf_op jit(solution)/shard_map/places/pallas_call | solution.py:479
  1.8 103.2 %sparse_product.1 = (bf16[1024,256]{1,0:T(8,128)(2,1)S(1)}, s32[1]{0:T(128)}) custom-call(bf16[1024,2048]{1,0:T(8,128)(2,1)} %left_ref.1, s32[16,32]{1,0:T(8,128)} %lpat_ref.1, bf16[2048,512]{1,0:T(8,128)(2,1)} %right_ref.1, s32[8,128]{1,0:T(8,128)} %get-tuple-element.25.code_ref, s32[8,128]{1,0:T(8,128)} %get-tuple-element.26.pack_ref), custom_call_target="tpu_custom_call" | custom-call | tf_op jit(solution)/shard_map/sparse_product/pallas_call | solution.py:441
  105.6 0.0 copy-done.7
  105.6 0.0 copy-done.6
  105.7 0.0 copy-done.1
  105.7 0.2 conditional.1
  105.9 0.8 copy.15
Async XLA Ops:
  0.0 105.6 %copy-start.7 = (s32[32,8]{0,1:T(8,128)S(1)}, s32[32,8]{0,1:T(8,128)}, u32[]{:S(2)}) copy-start(s32[32,8]{0,1:T(8,128)} %param.9) | copy-start | bytes 3076
  0.0 105.6 %copy-start.6 = (s32[16,32]{1,0:T(8,128)S(1)}, s32[16,32]{1,0:T(8,128)}, u32[]{:S(2)}) copy-start(s32[16,32]{1,0:T(8,128)} %lpat_ref.1) | copy-start | bytes 6148
  0.0 105.7 %copy-start.1 = (bf16[2048,512]{1,0:T(8,128)(2,1)S(1)}, bf16[2048,512]{1,0:T(8,128)(2,1)}, u32[]{:S(2)}) copy-start(bf16[2048,512]{1,0:T(8,128)(2,1)} %right_ref.1) | copy-start | bytes 6291460

commit v7 on v6

--- a/solution.py
+++ b/solution.py
@@ -11,9 +11,9 @@
 BLOCK = 64
 CAP = 148
 SPARE = 16
-EDGES = (0, 10, 20, 30, 40, 50, 58, 66, 74)
+EDGES = (0, 10, 20, 30, 40, 50, 56, 62, 66, 74)
 CHUNKS = len(EDGES) - 1
-READY = (3, 5, 7, 8)
+READY = (3, 5, 7, 9)
 LAG = 2
 
 
@@ -328,11 +328,12 @@
                       device(other(i), core))
 
     def add_cores(n):
-        for i in range(1, 5):
+        for k in range(1, 5):
+            i = jnp.where(lax.rem(chip, 2) == 1, k, k % 3 + 1) if k < 4 else 4
             q = other(i)
             swap(n, q).wait_recv()
             part[n, q, core] = part[n, q, core] + swapped[n, q]
-            if i < 4:
+            if k < 4:
                 scatter(n, i).start()
 
     def deliver(n, to, which, place, source, source_core):

time: 107 us -> 106 us (level)
  Pallas kernels: 105 us -> 103 us
    pallas_call x1, Pallas kernels: 103 us -> 102 us  [run(): pl.pallas_call(kernel, out_shape=(jax.ShapeDtypeStruct((rows, width // 2)...]
where the time goes in v7:
time: 106 us; the launch traced here: 105 us
  Pallas kernels  103 us (97%)
    pallas_call x1, Pallas kernels, run(): pl.pallas_call(kernel, out_shape=(jax.ShapeDtypeStruct((rows, width // 2)...  102 us

profile of v7, /device:TPU:0, one launch (start us, length us, event | category | flops | bytes accessed | tf_op | source)
XLA Modules:
  0.0 105.1 jit_solution(4582700422966298759)
XLA Ops:
  0.0 0.0 copy-start.7
  0.0 0.0 copy-start.6
  0.0 0.0 copy-start.1
  0.0 1.8 %places.1 = (s32[8,128]{1,0:T(8,128)}, s32[8,128]{1,0:T(8,128)}) custom-call(s32[8,32]{1,0:T(8,128)} %bitcast.14), custom_call_target="tpu_custom_call" | custom-call | tf_op jit(solution)/shard_map/places/pallas_call | solution.py:480
  1.8 101.6 %sparse_product.1 = (bf16[1024,256]{1,0:T(8,128)(2,1)S(1)}, s32[1]{0:T(128)}) custom-call(bf16[1024,2048]{1,0:T(8,128)(2,1)} %left_ref.1, s32[16,32]{1,0:T(8,128)} %lpat_ref.1, bf16[2048,512]{1,0:T(8,128)(2,1)} %right_ref.1, s32[8,128]{1,0:T(8,128)} %get-tuple-element.25.code_ref, s32[8,128]{1,0:T(8,128)} %get-tuple-element.26.pack_ref), custom_call_target="tpu_custom_call" | custom-call | tf_op jit(solution)/shard_map/sparse_product/pallas_call | solution.py:442
  104.0 0.0 copy-done.7
  104.1 0.0 copy-done.6
  104.1 0.0 copy-done.1
  104.1 0.2 conditional.1
  104.3 0.8 copy.15
Async XLA Ops:
  0.0 104.0 %copy-start.7 = (s32[32,8]{0,1:T(8,128)S(1)}, s32[32,8]{0,1:T(8,128)}, u32[]{:S(2)}) copy-start(s32[32,8]{0,1:T(8,128)} %param.9) | copy-start | bytes 3076
  0.0 104.1 %copy-start.6 = (s32[16,32]{1,0:T(8,128)S(1)}, s32[16,32]{1,0:T(8,128)}, u32[]{:S(2)}) copy-start(s32[16,32]{1,0:T(8,128)} %lpat_ref.1) | copy-start | bytes 6148
  0.0 104.1 %copy-start.1 = (bf16[2048,512]{1,0:T(8,128)(2,1)S(1)}, bf16[2048,512]{1,0:T(8,128)(2,1)}, u32[]{:S(2)}) copy-start(bf16[2048,512]{1,0:T(8,128)(2,1)} %right_ref.1) | copy-start | bytes 6291460
